TPU v7x, 32 devices: a whole 2x2x4 slice. The times are simulated.
32 devices in a mesh: row: 4 (over y, core), col: 2 (over x), blk: 4 (over z).
Axes of the slice: x: 2, y: 2, z: 4, core: 2. Of those that a mesh axis runs over, the one named last changes fastest.
Arguments:
- pixels: bfloat16 [256, 64, 1024], P('row', 'col', 'blk'), may hold values from -6 to 6
- dw_kernel: float32 [7, 7, 1024], P(None, None, 'blk'), may hold values from -4 to 4
- dw_bias: float32 [1024], P('blk'), may hold values from -3 to 3
- ln_gain: float32 [1024], P('blk'), may hold values from 0.25 to 1.75
- ln_bias: float32 [1024], P('blk'), may hold values from -2 to 2
- w_in: bfloat16 [4096, 1024], P('blk'), may hold values from -0.1875 to 0.1875
- b_in: bfloat16 [4096], P('blk'), may hold values from -2 to 2
- w_out: bfloat16 [4096, 1024], P('blk'), may hold values from -0.125 to 0.125
- b_out: float32 [1024], P('blk'), may hold values from -2 to 2
- layer_scale: float32 [1024], P('blk'), may hold values from 0.5 to 2
Outputs:
- block_out: bfloat16 [256, 64, 1024], P('row', 'col', 'blk')
All inputs are finite; a program needn't handle non-finite values.
Results may differ from a plain program's by a relative error of at most 0.012.
Values may be sent and summed in bfloat16 or wider, within the bound.
A program may use at most 64 MiB of HBM per device.

v0:
```python
import jax
import jax.numpy as jnp
from jax import lax
from jax.experimental import pallas as pl
from jax.experimental.pallas import tpu as pltpu
from jax.sharding import Mesh, PartitionSpec as P

KS = 7


def with_halo(cells, sides, width):
    for axis, dim in sides:
        count = lax.axis_size(axis)
        ends = count - 1
        head = lax.slice_in_dim(cells, 0, width, axis=dim)
        tail = lax.slice_in_dim(cells, cells.shape[dim] - width, cells.shape[dim], axis=dim)
        cells = jnp.concatenate(
            [
                lax.ppermute(tail, axis, [(i, (i + 1) % count) for i in range(ends)]),
                cells,
                lax.ppermute(head, axis, [((i + 1) % count, i) for i in range(ends)]),
            ],
            axis=dim,
        )
    return cells


def rotated(value, shift):
    count = lax.axis_size("blk")
    return lax.ppermute(value, "blk", [(i, (i + shift) % count) for i in range(count)])


def gathered(weights):
    half = weights.shape[0] // 2
    part = half // (lax.axis_size("y") * lax.axis_size("col"))
    place = lax.axis_index("y") * lax.axis_size("col") + lax.axis_index("col")
    own = lax.dynamic_slice_in_dim(
        weights, lax.axis_index("core") * half + place * part, part, axis=0
    )
    return lax.all_gather(own, ("blk", "y", "col"), axis=0, tiled=True)


def passed(w_in, b_in, w_out):
    chans = w_in.shape[1]
    half = w_in.shape[0] // 2
    plane = lax.axis_size("y") * lax.axis_size("col")
    part = half // plane
    start = lax.axis_index("core") * half
    place = lax.axis_index("y") * lax.axis_size("col") + lax.axis_index("col")
    begin = start + place * part
    bias_row = jnp.pad(
        lax.dynamic_slice_in_dim(b_in, begin, part)[None, :], ((0, 15), (0, chans - part))
    )
    own = jnp.concatenate(
        [
            lax.dynamic_slice_in_dim(w_in, begin, part, axis=0),
            lax.dynamic_slice_in_dim(w_out, begin, part, axis=0),
            bias_row,
        ]
    )
    pieces = []
    for k in range(1, lax.axis_size("blk")):
        arrived = rotated(own, k)
        pieces.append(arrived)
        for j in range(1, plane):
            pieces.append(lax.ppermute(arrived, ("y", "col"), [(i, i ^ j) for i in range(plane)]))
    w_first = [lax.dynamic_slice_in_dim(w_in, start, half, axis=0)] + [p[:part] for p in pieces]
    w_second = [lax.dynamic_slice_in_dim(w_out, start, half, axis=0)] + [
        p[part : 2 * part] for p in pieces
    ]
    bias = [lax.dynamic_slice_in_dim(b_in, start, half)] + [p[2 * part, :part] for p in pieces]
    return jnp.concatenate(w_first), jnp.concatenate(bias), jnp.concatenate(w_second)


def collected(w_in, b_in, w_out):
    half = b_in.shape[0] // 2
    b_first = lax.all_gather(
        lax.dynamic_slice_in_dim(b_in, lax.axis_index("core") * half, half),
        "blk",
        axis=0,
        tiled=True,
    )
    return gathered(w_in), b_first, gathered(w_out)


def mlp_kernel(own_ref, peer_ref, first_ref, bias_ref, second_ref, own_out, peer_out, total):
    step = pl.program_id(0)

    @pl.when(step == 0)
    def _():
        own_out[...] = jnp.zeros_like(own_out)
        total[...] = jnp.zeros_like(total)

    bias = bias_ref[...].astype(jnp.float32)
    for rows, sums in ((peer_ref, total), (own_ref, own_out)):
        pre_act = lax.dot_general(
            rows[...], first_ref[...], (((1,), (1,)), ((), ())), preferred_element_type=jnp.float32
        )
        pre_act = pre_act + bias
        hidden = 0.5 * pre_act * (1.0 + lax.erf(pre_act * 0.7071067811865476))
        sums[...] += jnp.dot(
            hidden.astype(jnp.bfloat16), second_ref[...], preferred_element_type=jnp.float32
        )

    @pl.when(step == pl.num_programs(0) - 1)
    def _():
        peer_out[...] = total[...].astype(peer_out.dtype)


def mlp_terms(own, peer, w_first, bias, w_second):
    count, chans = own.shape
    hid = w_first.shape[0]
    tile = min(1024, hid)
    whole = pl.BlockSpec((count, chans), lambda i: (0, 0))
    return pl.pallas_call(
        mlp_kernel,
        grid=(hid // tile,),
        in_specs=[
            whole,
            whole,
            pl.BlockSpec((tile, chans), lambda i: (i, 0)),
            pl.BlockSpec((1, tile), lambda i: (0, i)),
            pl.BlockSpec((tile, chans), lambda i: (i, 0)),
        ],
        out_specs=[whole, whole],
        out_shape=[
            jax.ShapeDtypeStruct((count, chans), jnp.float32),
            jax.ShapeDtypeStruct((count, chans), jnp.bfloat16),
        ],
        scratch_shapes=[pltpu.VMEM((count, chans), jnp.float32)],
        compiler_params=pltpu.CompilerParams(vmem_limit_bytes=48 * 1024 * 1024),
        cost_estimate=pl.CostEstimate(
            flops=8 * count * chans * hid, bytes_accessed=16 * count * chans, transcendentals=0
        ),
    )(own, peer, w_first, bias, w_second)


def shards(pixels, dw_kernel, dw_bias, ln_gain, ln_bias, w_in, b_in, w_out, b_out, layer_scale):
    tile_rows, tile_cols, chans = pixels.shape
    reach = (KS - 1) // 2
    blks = lax.axis_size("blk")
    plane = lax.axis_size("y") * lax.axis_size("col")
    few = plane in (1, 2, 4) and blks * plane <= 32
    w_first, b_first, w_second = (passed if few else collected)(w_in, b_in, w_out)
    padded = with_halo(pixels, ((("y", "core"), 0), ("col", 1)), reach).astype(jnp.float32)
    conv_out = jnp.zeros((tile_rows, tile_cols, chans), jnp.float32) + dw_bias
    for row_off in range(KS):
        for col_off in range(KS):
            conv_out = (
                conv_out
                + padded[row_off : row_off + tile_rows, col_off : col_off + tile_cols, :]
                * dw_kernel[row_off, col_off]
            )
    part_mean = jnp.mean(conv_out, axis=-1)
    off = conv_out - part_mean[..., None]
    part_sq = jnp.sum(off * off, axis=-1)
    stats = jnp.stack([part_mean, part_sq])
    everyone = [stats] + [rotated(stats, k) for k in range(1, blks)]
    mean = sum(s[0] for s in everyone) / blks
    sq = sum(s[1] + chans * (s[0] - mean) ** 2 for s in everyone)
    spread = sq / (chans * blks)
    normed = (
        (conv_out - mean[..., None]) * lax.rsqrt(spread + 1e-06)[..., None] * ln_gain + ln_bias
    ).astype(jnp.bfloat16)
    pixel_count = tile_rows * tile_cols
    own_px = pixel_count // blks
    flat = normed.reshape(blks, own_px, chans)
    regrouped = lax.all_to_all(flat.reshape(pixel_count, chans), "blk", split_axis=0, concat_axis=1, tiled=True)
    swap = [(0, 1), (1, 0)]
    peer = lax.ppermute(regrouped, "core", swap)
    kept, sent = mlp_terms(regrouped, peer, w_first, b_first[None, :], w_second)
    mlp = kept + lax.ppermute(sent, "core", swap).astype(jnp.float32)
    mlp = mlp.astype(jnp.bfloat16)
    summed = lax.all_to_all(mlp, "blk", split_axis=1, concat_axis=0, tiled=True)
    result = pixels.astype(jnp.float32) + layer_scale * (
        summed.astype(jnp.float32).reshape(tile_rows, tile_cols, chans) + b_out
    )
    return result.astype(jnp.bfloat16)


def solution(mesh):
    row, col, blk = (mesh.shape[name] for name in ("row", "col", "blk"))
    split = Mesh(mesh.devices.reshape(row // 2, 2, col, blk), ("y", "core", "col", "blk"))
    placed = (
        P(("y", "core"), "col", "blk"),
        P(None, None, "blk"),
        P("blk"),
        P("blk"),
        P("blk"),
        P("blk", None),
        P("blk"),
        P("blk", None),
        P("blk"),
        P("blk"),
    )
    return jax.shard_map(
        shards, mesh=split, in_specs=placed, out_specs=P(("y", "core"), "col", "blk"), check_vma=False
    )
```

profile of v0, /device:TPU:0, one launch (start us, length us, event | category | flops | bytes accessed | tf_op | source)
XLA Modules:
  0.0 191.7 jit_solution(2033555783639800869)
XLA Ops:
  0.0 0.8 dynamic-slice_bitcast_fusion
  0.8 1.1 constant_dynamic-slice_fusion
  1.9 0.9 fusion.50
  2.8 3.0 %collective-permute-start.8 = (bf16[272,1024]{1,0:T(8,128)(2,1)}, bf16[272,1024]{1,0:T(8,128)(2,1)}, u32[]{:S(2)}, u32[]{:S(2)}) collective-permute-start(bf16[272,1024]{1,0:T(8,128)(2,1)} %fusion.50), channel_id=1, source_target_pairs={{0,1},{1,2},{2,3},{3,0},{4,5},{5,6},{6,7},{7,4},{8,9},{9,10},{10,1... | collective-permute-start | bytes 1671176 | tf_op jit(solution)/shard_map/ppermute | solution.py:30
  5.8 2.6 %collective-permute-start.12 = (bf16[272,1024]{1,0:T(8,128)(2,1)}, bf16[272,1024]{1,0:T(8,128)(2,1)}, u32[]{:S(2)}, u32[]{:S(2)}) collective-permute-start(bf16[272,1024]{1,0:T(8,128)(2,1)} %fusion.50), channel_id=1, source_target_pairs={{0,2},{1,3},{2,0},{3,1},{4,6},{5,7},{6,4},{7,5},{8,10},{9,11},{10,... | collective-permute-start | bytes 1671176 | tf_op jit(solution)/shard_map/ppermute | solution.py:30
  8.4 1.3 collective-permute-start
  9.7 1.3 collective-permute-start.1
  11.7 2.8 %collective-permute-done.1 = bf16[3,32,256]{2,1,0:T(8,128)(2,1)S(1)} collective-permute-done((bf16[3,32,256]{2,1,0:T(8,128)(2,1)S(1)}, bf16[3,32,256]{2,1,0:T(8,128)(2,1)S(1)}, u32[]{:S(2)}, u32[]{:S(2)}) %collective-permute-start.1) | collective-permute-done | bytes 49184 | tf_op jit(solution)/shard_map/ppermute | solution.py:21
  14.7 3.4 %collective-permute-start.2 = (bf16[70,3,256]{2,1,0:T(4,128)(2,1)S(1)}, bf16[70,3,256]{2,1,0:T(4,128)(2,1)S(1)}, u32[]{:S(2)}, u32[]{:S(2)}) collective-permute-start(bf16[70,3,256]{2,1,0:T(4,128)(2,1)S(1)} %get-tuple-element.13), channel_id=1, source_target_pairs={{0,4},{1,5},{2,6},{3,7},{8,12},{9,13},{10,14},{11,15},{16,20},{17,... | collective-permute-start | bytes 322568 | tf_op jit(solution)/shard_map/ppermute | solution.py:19
  18.1 1.3 collective-permute-start.3
  20.0 0.7 collective-permute-done.2
  20.7 4.4 %collective-permute-done.3 = bf16[70,3,256]{2,1,0:T(4,128)(2,1)S(1)} collective-permute-done((bf16[70,3,256]{2,1,0:T(4,128)(2,1)S(1)}, bf16[70,3,256]{2,1,0:T(4,128)(2,1)S(1)}, u32[]{:S(2)}, u32[]{:S(2)}) %collective-permute-start.3) | collective-permute-done | bytes 107552 | tf_op jit(solution)/shard_map/ppermute | solution.py:21
  25.7 16.5 %fusion.61 = (f32[64,32]{1,0:T(8,128)S(1)}, f32[64,32,256]{2,1,0:T(8,128)S(1)}) fusion(f32[256]{0:T(256)} %bitcast.192, f32[70,38,256]{2,1,0:T(8,128)S(1)} %maximum_convert_fusion, f32[256]{0:T(256)} %bitcast.193, f32[256]{0:T(256)S(1)} %bitcast.146, f32[256]{0:T(256)S(1)} %bitcast.147, f32[256]{0:T(256)S(1)} %bitcast.148, f32[256]{0:T(256)S(1)} %bitcast.149, ...), kind=kLoop, calls=%fused_computation.170 | loop fusion | flops 51902464 | bytes 104916992 | tf_op jit(solution)/shard_map/reduce_sum | solution.py:154
  43.2 1.7 collective-permute-start.5
  44.9 1.9 collective-permute-start.6
  46.8 2.7 %dynamic-slice_dynamic-update-slice_fusion = (bf16[2048,1024]{1,0:T(8,128)(2,1)}, bf16[2048,1024]{1,0:T(8,128)(2,1)}) fusion(bf16[1024,1024]{1,0:T(8,128)(2,1)S(1)} %copy-done.2, s32[]{:T(128)S(6)} %select_n.4, bf16[1024,1024]{1,0:T(8,128)(2,1)} %param.15), kind=kLoop, calls=%fused_computation.106 | loop fusion | bytes 4194308
  49.8 0.8 collective-permute-start.16
  51.4 1.5 add_convert_fusion.2
  52.9 4.6 %all-to-all-start = ((bf16[4,512,256]{2,1,0:T(8,128)(2,1)}), bf16[4,512,256]{2,1,0:T(8,128)(2,1)S(1)}, u32[]{:S(2)}, u32[]{:S(2)}) async-start(bf16[4,512,256]{2,1,0:T(8,128)(2,1)} %bitcast.57), calls=%async_computation | async-start | bytes 2097152 | tf_op jit(solution)/shard_map/all_to_all | solution.py:168
  58.4 10.3 %collective-permute-start.10 = (bf16[272,1024]{1,0:T(8,128)(2,1)}, bf16[272,1024]{1,0:T(8,128)(2,1)S(1)}, u32[]{:S(2)}, u32[]{:S(2)}) collective-permute-start(bf16[272,1024]{1,0:T(8,128)(2,1)} %collective-permute-done.8), channel_id=1, source_target_pairs={{0,16},{4,20},{16,0},{20,4},{1,17},{5,21},{17,1},{21,5},{2,18},{6,... | collective-permute-start | bytes 1671176 | tf_op jit(solution)/shard_map/ppermute | solution.py:66
  68.7 1.4 collective-permute-start.11
  70.7 0.7 slice_bitcast_fusion.13
  71.4 1.9 slice_dynamic-update-slice_fusion.11
  73.2 1.5 collective-permute-start.14
  74.8 0.7 slice_bitcast_fusion.9
  75.5 8.4 %collective-permute-start.15 = (bf16[272,1024]{1,0:T(8,128)(2,1)}, bf16[272,1024]{1,0:T(8,128)(2,1)S(1)}, u32[]{:S(2)}, u32[]{:S(2)}) collective-permute-start(bf16[272,1024]{1,0:T(8,128)(2,1)} %collective-permute-done.12), channel_id=1, source_target_pairs={{0,20},{4,16},{16,4},{20,0},{1,21},{5,17},{17,5},{21,1},{2,22},{6,... | collective-permute-start | bytes 1671176 | tf_op jit(solution)/shard_map/ppermute | solution.py:66
  83.9 0.8 slice_dynamic-update-slice_fusion.10
  84.7 9.4 %collective-permute-done.10 = bf16[272,1024]{1,0:T(8,128)(2,1)S(1)} collective-permute-done((bf16[272,1024]{1,0:T(8,128)(2,1)}, bf16[272,1024]{1,0:T(8,128)(2,1)S(1)}, u32[]{:S(2)}, u32[]{:S(2)}) %collective-permute-start.10) | collective-permute-done | bytes 557088 | tf_op jit(solution)/shard_map/ppermute | solution.py:66
  94.1 2.3 %collective-permute-start.17 = (bf16[272,1024]{1,0:T(8,128)(2,1)}, bf16[272,1024]{1,0:T(8,128)(2,1)S(1)}, u32[]{:S(2)}, u32[]{:S(2)}) collective-permute-start(bf16[272,1024]{1,0:T(8,128)(2,1)} %collective-permute-done.16), channel_id=1, source_target_pairs={{0,4},{4,0},{16,20},{20,16},{1,5},{5,1},{17,21},{21,17},{2,6},{6,2... | collective-permute-start | bytes 1671176 | tf_op jit(solution)/shard_map/ppermute | solution.py:66
  97.0 0.8 slice_dynamic-update-slice_fusion.9
  98.0 9.8 %collective-permute-start.19 = (bf16[272,1024]{1,0:T(8,128)(2,1)}, bf16[272,1024]{1,0:T(8,128)(2,1)}, u32[]{:S(2)}, u32[]{:S(2)}) collective-permute-start(bf16[272,1024]{1,0:T(8,128)(2,1)} %collective-permute-done.16), channel_id=1, source_target_pairs={{0,20},{4,16},{16,4},{20,0},{1,21},{5,17},{17,5},{21,1},{2,22},{6,... | collective-permute-start | bytes 1671176 | tf_op jit(solution)/shard_map/ppermute | solution.py:66
  107.8 10.5 %collective-permute-done.14 = bf16[272,1024]{1,0:T(8,128)(2,1)S(1)} collective-permute-done((bf16[272,1024]{1,0:T(8,128)(2,1)}, bf16[272,1024]{1,0:T(8,128)(2,1)S(1)}, u32[]{:S(2)}, u32[]{:S(2)}) %collective-permute-start.14) | collective-permute-done | bytes 557088 | tf_op jit(solution)/shard_map/ppermute | solution.py:66
  118.3 0.8 slice_dynamic-update-slice_fusion.8
  119.1 2.8 %collective-permute-done.17 = bf16[272,1024]{1,0:T(8,128)(2,1)S(1)} collective-permute-done((bf16[272,1024]{1,0:T(8,128)(2,1)}, bf16[272,1024]{1,0:T(8,128)(2,1)S(1)}, u32[]{:S(2)}, u32[]{:S(2)}) %collective-permute-start.17) | collective-permute-done | bytes 557088 | tf_op jit(solution)/shard_map/ppermute | solution.py:66
  121.9 1.9 slice_dynamic-update-slice_fusion.7
  123.8 0.8 slice_dynamic-update-slice_fusion.6
  124.6 8.5 %collective-permute-done.18 = bf16[272,1024]{1,0:T(8,128)(2,1)S(1)} collective-permute-done((bf16[272,1024]{1,0:T(8,128)(2,1)}, bf16[272,1024]{1,0:T(8,128)(2,1)S(1)}, u32[]{:S(2)}, u32[]{:S(2)}) %collective-permute-start.18) | collective-permute-done | bytes 557088 | tf_op jit(solution)/shard_map/ppermute | solution.py:66
  133.0 0.8 slice_dynamic-update-slice_fusion.5
  133.9 0.8 slice_dynamic-update-slice_fusion.4
  137.7 1.9 slice_dynamic-update-slice_fusion.3
  139.6 0.9 slice_dynamic-update-slice_fusion.2
  140.5 0.9 slice_dynamic-update-slice_fusion.1
  141.3 1.9 slice_dynamic-update-slice_fusion
  143.2 11.9 %shard_map.100 = (f32[512,1024]{1,0:T(8,128)S(1)}, bf16[512,1024]{1,0:T(8,128)(2,1)S(1)}) custom-call(bf16[512,1024]{1,0:T(8,128)(2,1)S(1)} %bitcast.139, bf16[512,1024]{1,0:T(8,128)(2,1)S(1)} %collective-permute-done.7.peer_ref, bf16[2048,1024]{1,0:T(8,128)(2,1)} %get-tuple-element.18.first_ref, bf16[1,2048]{1,0:T(2,128)(2,1)S(1)} %broadcast_in_dim.5.bias_ref, ...), custom_call_target="tpu_custom_call" | custom-call | flops 8589934592 | bytes 8388608 | tf_op jit(solution)/shard_map/pallas_call | solution.py:115
  155.7 2.3 %collective-permute-done.20 = bf16[512,1024]{1,0:T(8,128)(2,1)S(1)} collective-permute-done((bf16[512,1024]{1,0:T(8,128)(2,1)S(1)}, bf16[512,1024]{1,0:T(8,128)(2,1)S(1)}, u32[]{:S(2)}, u32[]{:S(2)}) %collective-permute-start.20) | collective-permute-done | bytes 1048608 | tf_op jit(solution)/shard_map/ppermute | solution.py:172
  158.4 30.7 %all_to_all.32 = bf16[512,4,256]{2,0,1:T(8,128)(2,1)S(1)} all-to-all(bf16[512,4,256]{2,0,1:T(8,128)(2,1)S(1)} %bitcast.142), channel_id=1, replica_groups=mesh['y'=2,'core'=2,'col'=2,'blk'=4] {'blk'}, dimensions={1} | all-to-all | bytes 2097152 | tf_op jit(solution)/shard_map/all_to_all | solution.py:174
  189.3 1.0 copy-done.1
  190.3 1.4 add_convert_fusion
  (80 shorter events, 10.4 us)
Async XLA Ops:
  0.0 8.4 %copy-start = (bf16[64,32,256]{2,1,0:T(8,128)(2,1)S(1)}, bf16[64,32,256]{2,1,0:T(8,128)(2,1)}, u32[]{:S(2)}) copy-start(bf16[64,32,256]{2,1,0:T(8,128)(2,1)} %param.10) | copy-start | bytes 3145732
  0.0 11.0 %copy-start.3 = (f32[7,7,256]{2,1,0:T(8,128)S(1)}, f32[7,7,256]{2,1,0:T(8,128)}, u32[]{:S(2)}) copy-start(f32[7,7,256]{2,1,0:T(8,128)} %param.11) | copy-start | bytes 150532
  2.8 54.7 %collective-permute-start.8 = (bf16[272,1024]{1,0:T(8,128)(2,1)}, bf16[272,1024]{1,0:T(8,128)(2,1)}, u32[]{:S(2)}, u32[]{:S(2)}) collective-permute-start(bf16[272,1024]{1,0:T(8,128)(2,1)} %fusion.50), channel_id=1, source_target_pairs={{0,1},{1,2},{2,3},{3,0},{4,5},{5,6},{6,7},{7,4},{8,9},{9,10},{10,1... | collective-permute-start | bytes 1671176 | tf_op jit(solution)/shard_map/ppermute | solution.py:30
  5.8 64.3 %collective-permute-start.12 = (bf16[272,1024]{1,0:T(8,128)(2,1)}, bf16[272,1024]{1,0:T(8,128)(2,1)}, u32[]{:S(2)}, u32[]{:S(2)}) collective-permute-start(bf16[272,1024]{1,0:T(8,128)(2,1)} %fusion.50), channel_id=1, source_target_pairs={{0,2},{1,3},{2,0},{3,1},{4,6},{5,7},{6,4},{7,5},{8,10},{9,11},{10,... | collective-permute-start | bytes 1671176 | tf_op jit(solution)/shard_map/ppermute | solution.py:30
  8.4 3.2 %collective-permute-start = (bf16[3,32,256]{2,1,0:T(8,128)(2,1)S(1)}, bf16[3,32,256]{2,1,0:T(8,128)(2,1)S(1)}, u32[]{:S(2)}, u32[]{:S(2)}) collective-permute-start(bf16[3,32,256]{2,1,0:T(8,128)(2,1)S(1)} %get-tuple-element.16), channel_id=1, source_target_pairs={{0,8},{8,16},{16,24},{1,9},{9,17},{17,25},{2,10},{10,18},{18,26},{... | collective-permute-start | bytes 147464 | tf_op jit(solution)/shard_map/ppermute | solution.py:19
  9.7 4.9 %collective-permute-start.1 = (bf16[3,32,256]{2,1,0:T(8,128)(2,1)S(1)}, bf16[3,32,256]{2,1,0:T(8,128)(2,1)S(1)}, u32[]{:S(2)}, u32[]{:S(2)}) collective-permute-start(bf16[3,32,256]{2,1,0:T(8,128)(2,1)S(1)} %get-tuple-element.15), channel_id=1, source_target_pairs={{8,0},{16,8},{24,16},{9,1},{17,9},{25,17},{10,2},{18,10},{26,18},{... | collective-permute-start | bytes 147464 | tf_op jit(solution)/shard_map/ppermute | solution.py:21
  14.7 6.0 %collective-permute-start.2 = (bf16[70,3,256]{2,1,0:T(4,128)(2,1)S(1)}, bf16[70,3,256]{2,1,0:T(4,128)(2,1)S(1)}, u32[]{:S(2)}, u32[]{:S(2)}) collective-permute-start(bf16[70,3,256]{2,1,0:T(4,128)(2,1)S(1)} %get-tuple-element.13), channel_id=1, source_target_pairs={{0,4},{1,5},{2,6},{3,7},{8,12},{9,13},{10,14},{11,15},{16,20},{17,... | collective-permute-start | bytes 322568 | tf_op jit(solution)/shard_map/ppermute | solution.py:19
  18.1 7.0 %collective-permute-start.3 = (bf16[70,3,256]{2,1,0:T(4,128)(2,1)S(1)}, bf16[70,3,256]{2,1,0:T(4,128)(2,1)S(1)}, u32[]{:S(2)}, u32[]{:S(2)}) collective-permute-start(bf16[70,3,256]{2,1,0:T(4,128)(2,1)S(1)} %get-tuple-element.14), channel_id=1, source_target_pairs={{4,0},{5,1},{6,2},{7,3},{12,8},{13,9},{14,10},{15,11},{20,16},{21,... | collective-permute-start | bytes 322568 | tf_op jit(solution)/shard_map/ppermute | solution.py:21
  42.2 4.6 %copy-start.2 = (bf16[1024,1024]{1,0:T(8,128)(2,1)S(1)}, bf16[1024,1024]{1,0:T(8,128)(2,1)}, u32[]{:S(2)}) copy-start(bf16[1024,1024]{1,0:T(8,128)(2,1)} %param.17) | copy-start | bytes 6291460
  42.9 6.6 %copy-start.8 = (bf16[1024]{0:T(1024)(128)(2,1)S(1)}, bf16[1024]{0:T(1024)(128)(2,1)}, u32[]{:S(2)}) copy-start(bf16[1024]{0:T(1024)(128)(2,1)} %param.16) | copy-start | bytes 6148
  42.9 8.4 %copy-start.4 = (f32[256]{0:T(256)S(1)}, f32[256]{0:T(256)}, u32[]{:S(2)}) copy-start(f32[256]{0:T(256)} %param.14) | copy-start | bytes 3076
  42.9 8.4 %copy-start.5 = (f32[256]{0:T(256)S(1)}, f32[256]{0:T(256)}, u32[]{:S(2)}) copy-start(f32[256]{0:T(256)} %param.13) | copy-start | bytes 3076
  43.0 6.9 %collective-permute-start.4 = (f32[2,64,32]{2,1,0:T(8,128)S(1)}, f32[2,64,32]{2,1,0:T(8,128)S(1)}, u32[]{:S(2)}, u32[]{:S(2)}) collective-permute-start(f32[2,64,32]{2,1,0:T(8,128)S(1)} %pad_maximum_fusion), channel_id=1, source_target_pairs={{0,1},{1,2},{2,3},{3,0},{4,5},{5,6},{6,7},{7,4},{8,9},{9,10},{10,1... | collective-permute-start | bytes 49160 | tf_op jit(solution)/shard_map/ppermute | solution.py:30
  43.2 7.4 %collective-permute-start.5 = (f32[2,64,32]{2,1,0:T(8,128)S(1)}, f32[2,64,32]{2,1,0:T(8,128)S(1)}, u32[]{:S(2)}, u32[]{:S(2)}) collective-permute-start(f32[2,64,32]{2,1,0:T(8,128)S(1)} %pad_maximum_fusion), channel_id=1, source_target_pairs={{0,2},{1,3},{2,0},{3,1},{4,6},{5,7},{6,4},{7,5},{8,10},{9,11},{10,... | collective-permute-start | bytes 49160 | tf_op jit(solution)/shard_map/ppermute | solution.py:30
  44.9 6.4 %collective-permute-start.6 = (f32[2,64,32]{2,1,0:T(8,128)S(1)}, f32[2,64,32]{2,1,0:T(8,128)S(1)}, u32[]{:S(2)}, u32[]{:S(2)}) collective-permute-start(f32[2,64,32]{2,1,0:T(8,128)S(1)} %pad_maximum_fusion), channel_id=1, source_target_pairs={{0,3},{1,0},{2,1},{3,2},{4,7},{5,4},{6,5},{7,6},{8,11},{9,8},{10,9... | collective-permute-start | bytes 49160 | tf_op jit(solution)/shard_map/ppermute | solution.py:30
  49.8 23.4 %collective-permute-start.16 = (bf16[272,1024]{1,0:T(8,128)(2,1)}, bf16[272,1024]{1,0:T(8,128)(2,1)}, u32[]{:S(2)}, u32[]{:S(2)}) collective-permute-start(bf16[272,1024]{1,0:T(8,128)(2,1)} %fusion.50), channel_id=1, source_target_pairs={{0,3},{1,0},{2,1},{3,2},{4,7},{5,4},{6,5},{7,6},{8,11},{9,8},{10,9... | collective-permute-start | bytes 1671176 | tf_op jit(solution)/shard_map/ppermute | solution.py:30
  52.9 81.8 %all-to-all-start = ((bf16[4,512,256]{2,1,0:T(8,128)(2,1)}), bf16[4,512,256]{2,1,0:T(8,128)(2,1)S(1)}, u32[]{:S(2)}, u32[]{:S(2)}) async-start(bf16[4,512,256]{2,1,0:T(8,128)(2,1)} %bitcast.57), calls=%async_computation | async-start | bytes 2097152 | tf_op jit(solution)/shard_map/all_to_all | solution.py:168
  58.4 17.1 %collective-permute-start.9 = (bf16[272,1024]{1,0:T(8,128)(2,1)}, bf16[272,1024]{1,0:T(8,128)(2,1)S(1)}, u32[]{:S(2)}, u32[]{:S(2)}) collective-permute-start(bf16[272,1024]{1,0:T(8,128)(2,1)} %collective-permute-done.8), channel_id=1, source_target_pairs={{0,4},{4,0},{16,20},{20,16},{1,5},{5,1},{17,21},{21,17},{2,6},{6,2... | collective-permute-start | bytes 1671176 | tf_op jit(solution)/shard_map/ppermute | solution.py:66
  58.4 35.7 %collective-permute-start.10 = (bf16[272,1024]{1,0:T(8,128)(2,1)}, bf16[272,1024]{1,0:T(8,128)(2,1)S(1)}, u32[]{:S(2)}, u32[]{:S(2)}) collective-permute-start(bf16[272,1024]{1,0:T(8,128)(2,1)} %collective-permute-done.8), channel_id=1, source_target_pairs={{0,16},{4,20},{16,0},{20,4},{1,17},{5,21},{17,1},{21,5},{2,18},{6,... | collective-permute-start | bytes 1671176 | tf_op jit(solution)/shard_map/ppermute | solution.py:66
  68.7 27.7 %collective-permute-start.11 = (bf16[272,1024]{1,0:T(8,128)(2,1)}, bf16[272,1024]{1,0:T(8,128)(2,1)S(1)}, u32[]{:S(2)}, u32[]{:S(2)}) collective-permute-start(bf16[272,1024]{1,0:T(8,128)(2,1)} %collective-permute-done.8), channel_id=1, source_target_pairs={{0,20},{4,16},{16,4},{20,0},{1,21},{5,17},{17,5},{21,1},{2,22},{6,... | collective-permute-start | bytes 1671176 | tf_op jit(solution)/shard_map/ppermute | solution.py:66
  70.1 27.9 %collective-permute-start.13 = (bf16[272,1024]{1,0:T(8,128)(2,1)}, bf16[272,1024]{1,0:T(8,128)(2,1)S(1)}, u32[]{:S(2)}, u32[]{:S(2)}) collective-permute-start(bf16[272,1024]{1,0:T(8,128)(2,1)} %collective-permute-done.12), channel_id=1, source_target_pairs={{0,4},{4,0},{16,20},{20,16},{1,5},{5,1},{17,21},{21,17},{2,6},{6,2... | collective-permute-start | bytes 1671176 | tf_op jit(solution)/shard_map/ppermute | solution.py:66
  73.2 45.0 %collective-permute-start.14 = (bf16[272,1024]{1,0:T(8,128)(2,1)}, bf16[272,1024]{1,0:T(8,128)(2,1)S(1)}, u32[]{:S(2)}, u32[]{:S(2)}) collective-permute-start(bf16[272,1024]{1,0:T(8,128)(2,1)} %collective-permute-done.12), channel_id=1, source_target_pairs={{0,16},{4,20},{16,0},{20,4},{1,17},{5,21},{17,1},{21,5},{2,18},{6,... | collective-permute-start | bytes 1671176 | tf_op jit(solution)/shard_map/ppermute | solution.py:66
  75.5 43.7 %collective-permute-start.15 = (bf16[272,1024]{1,0:T(8,128)(2,1)}, bf16[272,1024]{1,0:T(8,128)(2,1)S(1)}, u32[]{:S(2)}, u32[]{:S(2)}) collective-permute-start(bf16[272,1024]{1,0:T(8,128)(2,1)} %collective-permute-done.12), channel_id=1, source_target_pairs={{0,20},{4,16},{16,4},{20,0},{1,21},{5,17},{17,5},{21,1},{2,22},{6,... | collective-permute-start | bytes 1671176 | tf_op jit(solution)/shard_map/ppermute | solution.py:66
  94.1 27.8 %collective-permute-start.17 = (bf16[272,1024]{1,0:T(8,128)(2,1)}, bf16[272,1024]{1,0:T(8,128)(2,1)S(1)}, u32[]{:S(2)}, u32[]{:S(2)}) collective-permute-start(bf16[272,1024]{1,0:T(8,128)(2,1)} %collective-permute-done.16), channel_id=1, source_target_pairs={{0,4},{4,0},{16,20},{20,16},{1,5},{5,1},{17,21},{21,17},{2,6},{6,2... | collective-permute-start | bytes 1671176 | tf_op jit(solution)/shard_map/ppermute | solution.py:66
  96.4 36.6 %collective-permute-start.18 = (bf16[272,1024]{1,0:T(8,128)(2,1)}, bf16[272,1024]{1,0:T(8,128)(2,1)S(1)}, u32[]{:S(2)}, u32[]{:S(2)}) collective-permute-start(bf16[272,1024]{1,0:T(8,128)(2,1)} %collective-permute-done.16), channel_id=1, source_target_pairs={{0,16},{4,20},{16,0},{20,4},{1,17},{5,21},{17,1},{21,5},{2,18},{6,... | collective-permute-start | bytes 1671176 | tf_op jit(solution)/shard_map/ppermute | solution.py:66
  98.0 36.9 %collective-permute-start.19 = (bf16[272,1024]{1,0:T(8,128)(2,1)}, bf16[272,1024]{1,0:T(8,128)(2,1)}, u32[]{:S(2)}, u32[]{:S(2)}) collective-permute-start(bf16[272,1024]{1,0:T(8,128)(2,1)} %collective-permute-done.16), channel_id=1, source_target_pairs={{0,20},{4,16},{16,4},{20,0},{1,21},{5,17},{17,5},{21,1},{2,22},{6,... | collective-permute-start | bytes 1671176 | tf_op jit(solution)/shard_map/ppermute | solution.py:66
  134.8 8.4 %collective-permute-start.7 = (bf16[512,1024]{1,0:T(8,128)(2,1)S(1)}, bf16[512,1024]{1,0:T(8,128)(2,1)S(1)}, u32[]{:S(2)}, u32[]{:S(2)}) collective-permute-start(bf16[512,1024]{1,0:T(8,128)(2,1)S(1)} %bitcast.138), channel_id=1, source_target_pairs={{0,8},{8,0},{1,9},{9,1},{2,10},{10,2},{3,11},{11,3},{4,12},{12,4},... | collective-permute-start | bytes 3145736 | tf_op jit(solution)/shard_map/ppermute | solution.py:170
  155.1 2.8 %collective-permute-start.20 = (bf16[512,1024]{1,0:T(8,128)(2,1)S(1)}, bf16[512,1024]{1,0:T(8,128)(2,1)S(1)}, u32[]{:S(2)}, u32[]{:S(2)}) collective-permute-start(bf16[512,1024]{1,0:T(8,128)(2,1)S(1)} %get-tuple-element.8), channel_id=1, source_target_pairs={{0,8},{8,0},{1,9},{9,1},{2,10},{10,2},{3,11},{11,3},{4,12},{12,4},... | collective-permute-start | bytes 3145736 | tf_op jit(solution)/shard_map/ppermute | solution.py:172
  189.1 1.2 copy-start.1
  189.1 1.2 copy-start.6
  189.1 1.2 copy-start.7
where the time goes:
time: 192 us
  starting transfers between devices  57.8 us (30%)
  waiting for transfers between devices  42.2 us (22%)
  blocking collectives  30.7 us (16%)
  local copies, waits for them, and re-layouts  26.8 us (14%)
  other arithmetic  22.1 us (12%)
  Pallas kernels  11.9 us (6%)
    ppermute x9, starting transfers between devices, passed(): lax.ppermute(arrived, ('y', 'col'), [(i, i ^ j) for i in range(plane)])  34.9 us
    ppermute x9, waiting for transfers between devices, passed(): lax.ppermute(arrived, ('y', 'col'), [(i, i ^ j) for i in range(plane)])  31.3 us
    all_to_all x1, blocking collectives, shards(): summed = lax.all_to_all(mlp, 'blk', split_axis=1, concat_axis=0, tiled=True)  30.7 us
    unnamed x44, local copies, waits for them, and re-layouts  18.4 us
    reduce_sum x1, other arithmetic, shards(): part_mean = jnp.mean(conv_out, axis=-1)  16.5 us
    pallas_call x1, Pallas kernels, mlp_terms(): pl.pallas_call(mlp_kernel, grid=(hid // tile,), in_specs=[whole, whole, p...  11.9 us
    ppermute x6, starting transfers between devices, rotated(): lax.ppermute(value, 'blk', [(i, (i + shift) % count) for i in range(count)])  10.3 us
    ppermute x2, waiting for transfers between devices, with_halo(): lax.ppermute(head, axis, [((i + 1) % count, i) for i in range(ends)])  7.22 us
  transfers between devices with their start and end apart: 22, of which 10 were waited for; matrix products, arithmetic and copies ran while one was open for 22% of the time, Pallas kernels for 0%

commit v1 on v0

--- a/solution.py
+++ b/solution.py
@@ -1,3 +1,4 @@
+import functools
 import jax
 import jax.numpy as jnp
 from jax import lax
@@ -135,7 +136,7 @@
     )(own, peer, w_first, bias, w_second)
 
 
-def shards(pixels, dw_kernel, dw_bias, ln_gain, ln_bias, w_in, b_in, w_out, b_out, layer_scale):
+def general(pixels, dw_kernel, dw_bias, ln_gain, ln_bias, w_in, b_in, w_out, b_out, layer_scale):
     tile_rows, tile_cols, chans = pixels.shape
     reach = (KS - 1) // 2
     blks = lax.axis_size("blk")
@@ -178,6 +179,548 @@
     return result.astype(jnp.bfloat16)
 
 
+REACH = (KS - 1) // 2
+PARTS = 4
+BLOCK = 128
+
+
+def fused_kernel(
+    px, dwk, dw_bias, gain, beta, b_in, w_in, w_out,
+    out,
+    pad, taps, conv, edge, edge_in, rows_in, corner_in, edge_f, stat, norm_stat, bias,
+    first, second, a_send, act, acc, p_send, p_in, r_send,
+    own_sem, halo_s, halo_r, bias_s, bias_r, stat_s, stat_r,
+    zown_s, zfwd_s, z_r, x_s, x_r, c_s, c_r,
+    a_s, a_r, a_l, y_s, y_r, p_s, p_r, r_s, r_r, r_l,
+):
+    tile_rows, tile_cols, chans = px.shape
+    blks = lax.axis_size("blk")
+    last_row = lax.axis_size("y") * 2 - 1
+    y, c, x, z = (lax.axis_index(name) for name in ("y", "core", "col", "blk"))
+    row = 2 * y + c
+    group_rows = tile_rows // blks
+    high, wide = group_rows + 2 * REACH, tile_cols + 2 * REACH
+    half = first.shape[1]
+    eighth = half // 4
+    part_rows = group_rows // PARTS
+    part_px = part_rows * tile_cols
+    part_regs = part_px * 8
+    stat_blocks = part_regs // BLOCK
+    full = blks * chans
+
+    def above(extra):
+        return {"y": (row - 1) // 2, "core": (row - 1) % 2, **extra}
+
+    def below(extra):
+        return {"y": (row + 1) // 2, "core": (row + 1) % 2, **extra}
+
+    def at_z(index):
+        return {"blk": index}
+
+    has_up, has_down = row > 0, row < last_row
+    side = {"col": 1 - x}
+    sibling = {"core": 1 - c}
+    partner = {"y": 1 - y}
+
+    def when(cond, act_fn):
+        if cond is None:
+            act_fn()
+        else:
+            pl.when(cond)(act_fn)
+
+    sent = []
+
+    def send(make, cond=None):
+        when(cond, lambda: make().start())
+        sent.append((make, cond))
+
+    def remote(src, dst, send_sem, recv_sem, device):
+        return pltpu.make_async_remote_copy(
+            src_ref=src, dst_ref=dst, send_sem=send_sem, recv_sem=recv_sem,
+            device_id=device, device_id_type=pl.DeviceIdType.MESH,
+        )
+
+    def arrived(dst, send_sem, recv_sem, device):
+        remote(dst, dst, send_sem, recv_sem, device).wait_recv()
+
+    barrier = pltpu.get_barrier_semaphore()
+
+    def greet(device):
+        pl.semaphore_signal(barrier, inc=1, device_id=device, device_id_type=pl.DeviceIdType.MESH)
+
+    for device in (side, sibling, partner):
+        greet(device)
+    for step in range(1, blks):
+        greet(at_z((z + step) % blks))
+
+    @pl.when(has_up)
+    def _():
+        greet(above({}))
+        greet(above(side))
+
+    @pl.when(has_down)
+    def _():
+        greet(below({}))
+        greet(below(side))
+
+    pl.semaphore_wait(barrier, 2 + blks + 2 * jnp.where(has_up, 1, 0) + 2 * jnp.where(has_down, 1, 0))
+
+    send(lambda: remote(px.at[pl.ds(0, REACH)], rows_in.at[1], halo_s.at[0], halo_r.at[1], above({})), has_up)
+    send(
+        lambda: remote(
+            px.at[pl.ds(tile_rows - REACH, REACH)], rows_in.at[0], halo_s.at[1], halo_r.at[0], below({})
+        ),
+        has_down,
+    )
+
+    start = pl.multiple_of(y * half, half)
+    mine = pl.multiple_of(x * (half // 2) + c * eighth, eighth)
+    across = pl.multiple_of((1 - x) * (half // 2) + c * eighth, eighth)
+    weights = ((w_in, first), (w_out, second))
+    for k, (src, dst) in enumerate(weights):
+        piece = lambda src=src: src.at[pl.ds(pl.multiple_of(start + mine, eighth), eighth)]
+        for way, cond, step in ((0, z < blks - 1, 1), (1, z > 0, -1)):
+            send(
+                lambda k=k, way=way, step=step, piece=piece, dst=dst: remote(
+                    piece(), dst.at[z, pl.ds(mine, eighth)], zown_s.at[k, way], z_r.at[k, z], at_z(z + step)
+                ),
+                cond,
+            )
+    own = [
+        pltpu.make_async_copy(src.at[pl.ds(start, half)], dst.at[z], own_sem.at[k])
+        for k, (src, dst) in enumerate(weights)
+    ]
+    for copy in own:
+        copy.start()
+
+    bias[z] = jnp.broadcast_to(b_in[:, pl.ds(start, half)], (8, half))
+    for step in range(1, blks):
+        send(
+            lambda step=step: remote(
+                bias.at[z], bias.at[z], bias_s.at[step], bias_r.at[z], at_z((z + step) % blks)
+            )
+        )
+
+    def body(i, _):
+        pad[pl.ds(pl.multiple_of(i * 8 * wide, 8), 8 * wide), :] = jnp.zeros((8 * wide, 128), jnp.float32)
+        return 0
+
+    lax.fori_loop(0, high, body, 0)
+    edge_f[...] = jnp.zeros_like(edge_f)
+
+    def put_row(values, group, line):
+        for tile in range(2):
+            pad[pl.ds((line * wide + REACH) * 8 + 4 * tile + group, tile_cols, stride=8), :] = values[
+                :, tile * 128 : (tile + 1) * 128
+            ]
+
+    for group in range(blks):
+        low = REACH if group == 0 else 0
+        top = high - (REACH if group == blks - 1 else 0)
+
+        def body(line, _, group=group):
+            put_row(px[group * group_rows + line - REACH].astype(jnp.float32), group, line)
+            return 0
+
+        lax.fori_loop(low, top, body, 0)
+
+    take = jnp.where(x == 0, tile_cols, REACH)
+    for j in range(REACH):
+        for tile in range(2):
+            for group in range(blks):
+                edge[j, group * group_rows : (group + 1) * group_rows, tile * 128 : (tile + 1) * 128] = pad[
+                    pl.ds((REACH * wide + take + j) * 8 + 4 * tile + group, group_rows, stride=8 * wide), :
+                ].astype(jnp.bfloat16)
+    send(lambda: remote(edge, edge_in, halo_s.at[2], halo_r.at[2], side))
+    send(
+        lambda: remote(edge.at[:, pl.ds(0, 16)], corner_in.at[1], halo_s.at[3], halo_r.at[4], above(side)), has_up
+    )
+    send(
+        lambda: remote(
+            edge.at[:, pl.ds(tile_rows - 16, 16)], corner_in.at[0], halo_s.at[4], halo_r.at[3], below(side)
+        ),
+        has_down,
+    )
+
+    for i in range(KS):
+        for tile in range(2):
+            for group in range(4):
+                taps[pl.ds(i * KS * 8 + 4 * tile + group, KS, stride=8), :] = dwk[
+                    i, :, tile * 128 : (tile + 1) * 128
+                ]
+    upper = lax.broadcasted_iota(jnp.int32, (8, 128), 0) < 4
+
+    def tiled(ref):
+        return jnp.where(
+            upper, jnp.broadcast_to(ref[:, 0:128], (8, 128)), jnp.broadcast_to(ref[:, 128:256], (8, 128))
+        )
+
+    @pl.when(has_up)
+    def _():
+        arrived(rows_in.at[0], halo_s.at[0], halo_r.at[0], above({}))
+        for i in range(REACH):
+            put_row(rows_in[0, i].astype(jnp.float32), 0, i)
+
+    @pl.when(has_down)
+    def _():
+        arrived(rows_in.at[1], halo_s.at[1], halo_r.at[1], below({}))
+        for i in range(REACH):
+            put_row(rows_in[1, i].astype(jnp.float32), blks - 1, high - REACH + i)
+
+    arrived(edge_in, halo_s.at[2], halo_r.at[2], side)
+    for j in range(REACH):
+        for tile in range(2):
+            edge_f[j, tile, REACH : REACH + tile_rows, :] = edge_in[
+                j, :, tile * 128 : (tile + 1) * 128
+            ].astype(jnp.float32)
+
+    @pl.when(has_up)
+    def _():
+        arrived(corner_in.at[0], halo_s.at[3], halo_r.at[3], above(side))
+        for j in range(REACH):
+            for tile in range(2):
+                edge_f[j, tile, 0:REACH, :] = corner_in[0, j, :, tile * 128 : (tile + 1) * 128].astype(
+                    jnp.float32
+                )[16 - REACH :]
+
+    @pl.when(has_down)
+    def _():
+        arrived(corner_in.at[1], halo_s.at[4], halo_r.at[4], below(side))
+        for j in range(REACH):
+            for tile in range(2):
+                edge_f[j, tile, REACH + tile_rows : 2 * REACH + tile_rows, :] = corner_in[
+                    1, j, :, tile * 128 : (tile + 1) * 128
+                ].astype(jnp.float32)[:REACH]
+
+    place = jnp.where(x == 0, tile_cols + REACH, 0)
+    for j in range(REACH):
+        for tile in range(2):
+            for group in range(blks):
+                pad[pl.ds((place + j) * 8 + 4 * tile + group, high, stride=8 * wide), :] = edge_f[
+                    j, tile, group * group_rows : group * group_rows + high, :
+                ]
+
+    def convolve(part):
+        def body(i, _):
+            line = part * part_rows + i // (tile_cols // 8)
+            col = (i % (tile_cols // 8)) * 8
+            total = jnp.broadcast_to(tiled(dw_bias)[None], (8, 8, 128))
+            for up in range(KS):
+                begin = pl.multiple_of(((line + up) * wide + col) * 8, 8)
+                cells = pad[pl.ds(begin, 8 * (7 + KS)), :].reshape(7 + KS, 8, 128)
+                for j in range(KS):
+                    weight = taps[(up * KS + j) * 8 : (up * KS + j + 1) * 8, :]
+                    total = total + cells[j : j + 8] * weight[None]
+            conv[pl.ds(pl.multiple_of((line * tile_cols + col) * 8, 64), 64), :] = total.reshape(64, 128)
+            return 0
+
+        lax.fori_loop(0, part_px // 8, body, 0)
+
+    def both_tiles(values):
+        return values + pltpu.roll(values, 4, 1)
+
+    def measure(part):
+        def body(b, _):
+            cells = conv[pl.ds(pl.multiple_of(part * part_regs + b * BLOCK, BLOCK), BLOCK), :].reshape(
+                BLOCK // 8, 8, 128
+            )
+            sums = jnp.broadcast_to(jnp.sum(cells, axis=2, keepdims=True), cells.shape)
+            mean = both_tiles(sums) * (1.0 / chans)
+            off = cells - mean
+            squares = both_tiles(jnp.broadcast_to(jnp.sum(off * off, axis=2, keepdims=True), cells.shape))
+            lane = lax.broadcasted_iota(jnp.int32, cells.shape, 2)
+            turned = jnp.where(lane == 0, mean, squares).reshape(BLOCK, 128).T
+            stat[part, z, 0, pl.ds(b, 1), :] = turned[0:1]
+            stat[part, z, 1, pl.ds(b, 1), :] = turned[1:2]
+            return 0
+
+        lax.fori_loop(0, stat_blocks, body, 0)
+        for step in range(1, blks):
+            send(
+                lambda step=step: remote(
+                    stat.at[part, z], stat.at[part, z], stat_s.at[part, step], stat_r.at[part, z],
+                    at_z((z + step) % blks),
+                )
+            )
+
+    def columns(index):
+        return pl.ds(pl.multiple_of(index * chans, chans), chans)
+
+    def normalize(part):
+        for step in range(1, blks):
+            other = (z + step) % blks
+            arrived(stat.at[part, other], stat_s.at[part, step], stat_r.at[part, other], at_z(other))
+        mean = sum(stat[part, o, 0] for o in range(blks)) / blks
+        spread = sum(stat[part, o, 1] + chans * (stat[part, o, 0] - mean) ** 2 for o in range(blks)) / full
+        norm_stat[0] = mean
+        norm_stat[1] = lax.rsqrt(spread + 1e-06)
+
+        def body(b, _):
+            where = pl.ds(pl.multiple_of(part * part_regs + b * BLOCK, BLOCK), BLOCK)
+            cells = conv[where, :].reshape(BLOCK // 8, 8, 128)
+            means, scales = (
+                jnp.broadcast_to(norm_stat[k, pl.ds(b, 1), :], (BLOCK, 128)).T.reshape(BLOCK // 8, 8, 128)
+                for k in range(2)
+            )
+            normed = (cells - means) * scales * tiled(gain)[None] + tiled(beta)[None]
+            conv[where, :] = normed.reshape(BLOCK, 128)
+            return 0
+
+        lax.fori_loop(0, stat_blocks, body, 0)
+        for group in range(blks):
+            for tile in range(2):
+                a_send[part, group, :, tile * 128 : (tile + 1) * 128] = conv[
+                    pl.ds(part * part_regs + 4 * tile + group, part_px, stride=8), :
+                ].astype(jnp.bfloat16)
+        for step in range(1, blks):
+            send(
+                lambda step=step: remote(
+                    a_send.at[part, (z + step) % blks], act.at[part, pl.ds(0, part_px), columns(z)],
+                    a_s.at[part, step], a_r.at[part, z], at_z((z + step) % blks),
+                )
+            )
+        pltpu.make_async_copy(
+            a_send.at[part, z], act.at[part, pl.ds(0, part_px), columns(z)], a_l.at[part]
+        ).start()
+
+    def swap_rows(part):
+        for step in range(1, blks):
+            other = (z + step) % blks
+            arrived(
+                act.at[part, pl.ds(0, part_px), columns(other)], a_s.at[part, step], a_r.at[part, other], at_z(other)
+            )
+        pltpu.make_async_copy(
+            a_send.at[part, z], act.at[part, pl.ds(0, part_px), columns(z)], a_l.at[part]
+        ).wait()
+        send(
+            lambda: remote(
+                act.at[part, pl.ds(0, part_px)], act.at[part, pl.ds(part_px, part_px)],
+                y_s.at[part], y_r.at[part], partner,
+            )
+        )
+
+    def both_ways(dist):
+        return ((z >= dist, lambda: z - dist, z < blks - 1, 1), (z + dist < blks, lambda: z + dist, z > 0, -1))
+
+    def relay(dist, k):
+        block = weights[k][1]
+        for cond, origin, more, step in both_ways(dist):
+            spot = lambda origin=origin: block.at[origin(), pl.ds(mine, eighth)]
+            when(
+                cond,
+                lambda spot=spot, origin=origin: arrived(spot(), zown_s.at[k, 0], z_r.at[k, origin()], side),
+            )
+            if dist < blks - 1:
+                send(
+                    lambda spot=spot, origin=origin, step=step: remote(
+                        spot(), spot(), zfwd_s.at[k, origin()], z_r.at[k, origin()], at_z(z + step)
+                    ),
+                    cond & more,
+                )
+            send(
+                lambda spot=spot, origin=origin: remote(
+                    spot(), spot(), x_s.at[k, origin()], x_r.at[k, origin()], side
+                ),
+                cond,
+            )
+            send(
+                lambda spot=spot, origin=origin: remote(
+                    spot(), spot(), c_s.at[k, 0, origin()], c_r.at[k, 0, origin()], sibling
+                ),
+                cond,
+            )
+
+    def share(dist, k):
+        block = weights[k][1]
+        for cond, origin, _, _ in both_ways(dist):
+            spot = lambda origin=origin: block.at[origin(), pl.ds(across, eighth)]
+            when(
+                cond,
+                lambda spot=spot, origin=origin: arrived(
+                    spot(), x_s.at[k, origin()], x_r.at[k, origin()], side
+                ),
+            )
+            send(
+                lambda spot=spot, origin=origin: remote(
+                    spot(), spot(), c_s.at[k, 1, origin()], c_r.at[k, 1, origin()], sibling
+                ),
+                cond,
+            )
+
+    def ready():
+        for copy in own:
+            copy.wait()
+        for step in range(1, blks):
+            other = (z + step) % blks
+            arrived(bias.at[other], bias_s.at[step], bias_r.at[other], at_z(other))
+            for k in range(2):
+                for n, column in ((0, x), (1, 1 - x)):
+                    begin = pl.multiple_of(column * (half // 2) + (1 - c) * eighth, eighth)
+                    arrived(
+                        weights[k][1].at[other, pl.ds(begin, eighth)],
+                        c_s.at[k, n, other], c_r.at[k, n, other], sibling,
+                    )
+
+    def feed(part):
+        arrived(act.at[part, pl.ds(part_px, part_px)], y_s.at[part], y_r.at[part], partner)
+
+        def body(o, _):
+            pre_act = lax.dot_general(
+                act[part], first[o], (((1,), (1,)), ((), ())), preferred_element_type=jnp.float32
+            )
+            pre_act = pre_act + bias[o, 0:1, :]
+            hidden = 0.5 * pre_act * (1.0 + lax.erf(pre_act * 0.7071067811865476))
+            term = jnp.dot(hidden.astype(jnp.bfloat16), second[o], preferred_element_type=jnp.float32)
+
+            @pl.when(o == 0)
+            def _():
+                acc[part] = term
+
+            @pl.when(o > 0)
+            def _():
+                acc[part] += term
+
+            return 0
+
+        lax.fori_loop(0, blks, body, 0)
+        p_send[part] = acc[part, part_px:, :].astype(jnp.bfloat16)
+        send(lambda: remote(p_send.at[part], p_in.at[part], p_s.at[part], p_r.at[part], partner))
+
+    def result_rows(owner, part):
+        return out.at[pl.ds(pl.multiple_of(owner * (part_px * PARTS) + part * part_px, part_px), part_px)]
+
+    def give_back(part):
+        arrived(p_in.at[part], p_s.at[part], p_r.at[part], partner)
+        r_send[part] = (acc[part, :part_px, :] + p_in[part].astype(jnp.float32)).astype(jnp.bfloat16)
+        for step in range(1, blks):
+            send(
+                lambda step=step: remote(
+                    r_send.at[part, :, columns((z + step) % blks)], result_rows(z, part),
+                    r_s.at[part, step], r_r.at[part, z], at_z((z + step) % blks),
+                )
+            )
+        pltpu.make_async_copy(r_send.at[part, :, columns(z)], result_rows(z, part), r_l.at[part]).start()
+
+    def collect(part):
+        for step in range(1, blks):
+            other = (z + step) % blks
+            arrived(result_rows(other, part), r_s.at[part, step], r_r.at[part, other], at_z(other))
+        pltpu.make_async_copy(r_send.at[part, :, columns(z)], result_rows(z, part), r_l.at[part]).wait()
+
+    convolve(0)
+    measure(0)
+    relay(1, 0)
+    convolve(1)
+    measure(1)
+    normalize(0)
+    relay(1, 1)
+    share(1, 0)
+    convolve(2)
+    measure(2)
+    normalize(1)
+    relay(2, 0)
+    share(1, 1)
+    convolve(3)
+    measure(3)
+    normalize(2)
+    normalize(3)
+    relay(2, 1)
+    share(2, 0)
+    swap_rows(0)
+    relay(3, 0)
+    share(2, 1)
+    swap_rows(1)
+    relay(3, 1)
+    share(3, 0)
+    swap_rows(2)
+    share(3, 1)
+    ready()
+    feed(0)
+    swap_rows(3)
+    feed(1)
+    give_back(0)
+    feed(2)
+    give_back(1)
+    feed(3)
+    give_back(2)
+    give_back(3)
+    for part in range(PARTS):
+        collect(part)
+    for make, cond in sent:
+        when(cond, lambda make=make: make().wait_send())
+
+
+def fused(pixels, dw_kernel, dw_bias, ln_gain, ln_bias, w_in, b_in, w_out, b_out, layer_scale):
+    tile_rows, tile_cols, chans = pixels.shape
+    blks = lax.axis_size("blk")
+    full = blks * chans
+    half = w_in.shape[0] // 2
+    group_rows = tile_rows // blks
+    px = group_rows * tile_cols
+    part_px = px // PARTS
+    high, wide = group_rows + 2 * REACH, tile_cols + 2 * REACH
+    vmem, dma = pltpu.VMEM, pltpu.SemaphoreType.DMA
+    here = pl.BlockSpec(memory_space=pltpu.VMEM)
+    anywhere = pl.BlockSpec(memory_space=pl.ANY)
+    bf16, f32 = jnp.bfloat16, jnp.float32
+    summed = pl.pallas_call(
+        fused_kernel,
+        in_specs=[here] * 6 + [anywhere] * 2,
+        out_specs=anywhere,
+        out_shape=jax.ShapeDtypeStruct((tile_rows * tile_cols, chans), bf16),
+        scratch_shapes=[
+            vmem((high * wide * 8, 128), f32),
+            vmem((KS * KS * 8, 128), f32),
+            vmem((px * 8, 128), f32),
+            vmem((REACH, tile_rows, chans), bf16),
+            vmem((REACH, tile_rows, chans), bf16),
+            vmem((2, REACH, tile_cols, chans), bf16),
+            vmem((2, REACH, 16, chans), bf16),
+            vmem((REACH, 2, tile_rows + 8, 128), f32),
+            vmem((PARTS, blks, 2, 8, 128), f32),
+            vmem((2, 8, 128), f32),
+            vmem((blks, 8, half), f32),
+            vmem((blks, half, full), bf16),
+            vmem((blks, half, full), bf16),
+            vmem((PARTS, blks, part_px, chans), bf16),
+            vmem((PARTS, 2 * part_px, full), bf16),
+            vmem((PARTS, 2 * part_px, full), f32),
+            vmem((PARTS, part_px, full), bf16),
+            vmem((PARTS, part_px, full), bf16),
+            vmem((PARTS, part_px, full), bf16),
+            dma((2,)), dma((5,)), dma((5,)), dma((blks,)), dma((blks,)), dma((PARTS, blks)), dma((PARTS, blks)),
+            dma((2, 2)), dma((2, blks)), dma((2, blks)), dma((2, blks)), dma((2, blks)),
+            dma((2, 2, blks)), dma((2, 2, blks)),
+            dma((PARTS, blks)), dma((PARTS, blks)), dma((PARTS,)),
+            dma((PARTS,)), dma((PARTS,)), dma((PARTS,)), dma((PARTS,)),
+            dma((PARTS, blks)), dma((PARTS, blks)), dma((PARTS,)),
+        ],
+        compiler_params=pltpu.CompilerParams(
+            collective_id=0, has_side_effects=True, vmem_limit_bytes=48 * 1024 * 1024
+        ),
+    )(
+        pixels, dw_kernel, dw_bias[None, :], ln_gain[None, :], ln_bias[None, :],
+        b_in.astype(f32)[None, :], w_in, w_out,
+    )
+    result = pixels.astype(f32) + layer_scale * (
+        summed.astype(f32).reshape(tile_rows, tile_cols, chans) + b_out
+    )
+    return result.astype(bf16)
+
+
+def shards(pixels, *params):
+    tile_rows, tile_cols, chans = pixels.shape
+    blks = lax.axis_size("blk")
+    fits = (
+        (lax.axis_size("y"), lax.axis_size("col"), blks, chans) == (2, 2, 4, 256)
+        and tile_cols % 16 == 0
+        and tile_rows % (4 * blks) == 0
+        and tile_rows * tile_cols == blks * PARTS * BLOCK
+        and params[4].shape[0] % 1024 == 0
+    )
+    return (fused if fits else general)(pixels, *params)
+
+
 def solution(mesh):
     row, col, blk = (mesh.shape[name] for name in ("row", "col", "blk"))
     split = Mesh(mesh.devices.reshape(row // 2, 2, col, blk), ("y", "core", "col", "blk"))

time: 192 us -> 118 us (0.61)
  Pallas kernels: 11.9 us -> 110 us
  starting transfers between devices: 57.8 us -> 0 us
  waiting for transfers between devices: 42.2 us -> 0 us
  blocking collectives: 30.7 us -> 0 us
  local copies, waits for them, and re-layouts: 26.8 us -> 5.68 us
  other arithmetic: 22.1 us -> 2.1 us
    pallas_call x1, Pallas kernels: 11.9 us -> 110 us  [fused(): pl.pallas_call(fused_kernel, in_specs=[here] * 6 + [anywhere] * 2, out_sp...]
    ppermute x21 -> x0, starting transfers between devices: 53.1 us -> none  [the longest x9 34.9 us: passed(): lax.ppermute(arrived, ('y', 'col'), [(i, i ^ j) for i in range(plane)])]
    ppermute x21 -> x0, waiting for transfers between devices: 42.2 us -> none  [the longest x9 31.3 us: passed(): lax.ppermute(arrived, ('y', 'col'), [(i, i ^ j) for i in range(plane)])]
    all_to_all x1 -> x0, blocking collectives: 30.7 us -> none  [shards(): summed = lax.all_to_all(mlp, 'blk', split_axis=1, concat_axis=0, tiled=True)]
    reduce_sum x2 -> x0, other arithmetic: 17.1 us -> none  [the longest x1 16.5 us: shards(): part_mean = jnp.mean(conv_out, axis=-1)]
    unnamed x44 -> x16, local copies, waits for them, and re-layouts: 18.4 us -> 5.68 us
    all_to_all x1 -> x0, starting transfers between devices: 4.62 us -> none  [shards(): lax.all_to_all(flat.reshape(pixel_count, chans), 'blk', split_axis=0, con...]
    squeeze x12 -> x0, local copies, waits for them, and re-layouts: 2.73 us -> none  [passed(): p[2 * part, :part]]
  transfers between devices with their start and end apart: 22 -> 0, of which waited for: 10 -> 0; matrix products, arithmetic and copies ran while one was open for 22% -> 0% of each run, Pallas kernels for 0% -> 0%
where the time goes in v1:
time: 118 us
  Pallas kernels  110 us (93%)
  local copies, waits for them, and re-layouts  5.68 us (5%)
  other arithmetic  2.1 us (2%)
    pallas_call x1, Pallas kernels, fused(): pl.pallas_call(fused_kernel, in_specs=[here] * 6 + [anywhere] * 2, out_sp...  110 us
    unnamed x16, local copies, waits for them, and re-layouts  5.68 us

profile of v1, /device:TPU:0, one launch (start us, length us, event | category | flops | bytes accessed | tf_op | source)
XLA Modules:
  0.0 117.8 jit_solution(18440613668842375827)
XLA Ops:
  0.0 0.7 broadcast_in_dim.21
  0.7 0.0 copy-start
  0.7 1.2 %copy-done = bf16[64,32,256]{2,1,0:T(8,128)(2,1)S(1)} copy-done((bf16[64,32,256]{2,1,0:T(8,128)(2,1)S(1)}, bf16[64,32,256]{2,1,0:T(8,128)(2,1)}, u32[]{:S(2)}) %copy-start) | copy-done | bytes 1048600
  1.9 0.0 copy-start.1
  1.9 1.6 %copy-done.1 = bf16[1024,1024]{1,0:T(8,128)(2,1)S(1)} copy-done((bf16[1024,1024]{1,0:T(8,128)(2,1)S(1)}, bf16[1024,1024]{1,0:T(8,128)(2,1)}, u32[]{:S(2)}) %copy-start.1) | copy-done | bytes 2097176
  3.5 0.0 copy-start.2
  3.5 0.8 copy-done.2
  4.3 0.0 copy-start.3
  4.3 0.7 copy-done.3
  5.0 0.0 copy-start.4
  5.0 0.7 copy-done.4
  5.7 0.0 copy-start.5
  5.7 0.7 copy-done.5
  6.4 0.0 copy-start.6
  6.4 0.0 copy-start.7
  6.4 110.0 %shard_map.100 = bf16[2048,256]{1,0:T(8,128)(2,1)S(1)} custom-call(bf16[64,32,256]{2,1,0:T(8,128)(2,1)S(1)} %copy-done, f32[7,7,256]{2,1,0:T(8,128)S(1)} %copy-done.2, f32[1,256]{1,0:T(1,128)S(1)} %bitcast.8, f32[1,256]{1,0:T(1,128)S(1)} %bitcast.9, f32[1,256]{1,0:T(1,128)S(1)} %bitcast.10, f32[1,1024]{1,0:T(1,128)S(1)} %bitcast.7, ...), custom_call_target="tpu_custom_call" | custom-call | tf_op jit(solution)/shard_map/pallas_call | solution.py:666
  116.4 0.0 copy-done.6
  116.4 0.0 copy-done.7
  116.4 1.4 %fusion.2 = bf16[64,32,256]{2,1,0:T(8,128)(2,1)} fusion(bf16[64,32,256]{2,1,0:T(8,128)(2,1)S(1)} %bitcast.6, bf16[64,32,256]{2,1,0:T(8,128)(2,1)S(1)} %copy-done, f32[256]{0:T(256)S(1)} %copy-done.6, f32[256]{0:T(256)S(1)} %copy-done.7), kind=kLoop, calls=%fused_computation.3 | loop fusion | flops 3145728 | bytes 3147776 | tf_op jit(solution)/shard_map/convert_element_type | solution.py:708
Async XLA Ops:
  0.7 1.2 %copy-start = (bf16[64,32,256]{2,1,0:T(8,128)(2,1)S(1)}, bf16[64,32,256]{2,1,0:T(8,128)(2,1)}, u32[]{:S(2)}) copy-start(bf16[64,32,256]{2,1,0:T(8,128)(2,1)} %px.1) | copy-start | bytes 3145732
  1.9 1.6 %copy-start.1 = (bf16[1024,1024]{1,0:T(8,128)(2,1)S(1)}, bf16[1024,1024]{1,0:T(8,128)(2,1)}, u32[]{:S(2)}) copy-start(bf16[1024,1024]{1,0:T(8,128)(2,1)} %w_in.1) | copy-start | bytes 6291460
  3.5 0.8 copy-start.2
  4.3 0.7 copy-start.3
  5.0 0.7 copy-start.4
  5.7 0.7 copy-start.5
  6.4 110.0 %copy-start.6 = (f32[256]{0:T(256)S(1)}, f32[256]{0:T(256)}, u32[]{:S(2)}) copy-start(f32[256]{0:T(256)} %param.18) | copy-start | bytes 3076
  6.4 110.0 %copy-start.7 = (f32[256]{0:T(256)S(1)}, f32[256]{0:T(256)}, u32[]{:S(2)}) copy-start(f32[256]{0:T(256)} %param.19) | copy-start | bytes 3076

commit v2 on v1

--- a/solution.py
+++ b/solution.py
@@ -181,12 +181,15 @@
 
 REACH = (KS - 1) // 2
 PARTS = 4
+GROUPS = 8
 BLOCK = 128
+STATS = 4
 
 
 def fused_kernel(
-    px, dwk, dw_bias, gain, beta, b_in, w_in, w_out,
+    px_hbm, dwk_hbm, dw_bias_hbm, gain_hbm, beta_hbm, b_in_hbm, w_in, w_out,
     out,
+    px, dwk, dw_bias, gain, beta, b_in, b_wide, load_sem,
     pad, taps, conv, edge, edge_in, rows_in, corner_in, edge_f, stat, norm_stat, bias,
     first, second, a_send, act, acc, p_send, p_in, r_send,
     own_sem, halo_s, halo_r, bias_s, bias_r, stat_s, stat_r,
@@ -198,13 +201,15 @@
     last_row = lax.axis_size("y") * 2 - 1
     y, c, x, z = (lax.axis_index(name) for name in ("y", "core", "col", "blk"))
     row = 2 * y + c
-    group_rows = tile_rows // blks
-    high, wide = group_rows + 2 * REACH, tile_cols + 2 * REACH
+    lines = tile_rows // GROUPS
+    high, wide = lines + 2 * REACH, tile_cols + 2 * REACH
     half = first.shape[1]
     eighth = half // 4
-    part_rows = group_rows // PARTS
-    part_px = part_rows * tile_cols
-    part_regs = part_px * 8
+    per_blk = GROUPS // blks
+    part_rows = lines // PARTS
+    group_px = part_rows * tile_cols
+    part_px = per_blk * group_px
+    part_regs = group_px * GROUPS
     stat_blocks = part_regs // BLOCK
     full = blks * chans
 
@@ -243,6 +248,15 @@
     def arrived(dst, send_sem, recv_sem, device):
         remote(dst, dst, send_sem, recv_sem, device).wait_recv()
 
+    loads = [
+        pltpu.make_async_copy(src, dst, load_sem.at[k])
+        for k, (src, dst) in enumerate(
+            ((px_hbm, px), (dwk_hbm, dwk), (dw_bias_hbm, dw_bias), (gain_hbm, gain), (beta_hbm, beta), (b_in_hbm, b_in))
+        )
+    ]
+    for copy in loads:
+        copy.start()
+
     barrier = pltpu.get_barrier_semaphore()
 
     def greet(device):
@@ -265,10 +279,10 @@
 
     pl.semaphore_wait(barrier, 2 + blks + 2 * jnp.where(has_up, 1, 0) + 2 * jnp.where(has_down, 1, 0))
 
-    send(lambda: remote(px.at[pl.ds(0, REACH)], rows_in.at[1], halo_s.at[0], halo_r.at[1], above({})), has_up)
+    send(lambda: remote(px_hbm.at[pl.ds(0, REACH)], rows_in.at[1], halo_s.at[0], halo_r.at[1], above({})), has_up)
     send(
         lambda: remote(
-            px.at[pl.ds(tile_rows - REACH, REACH)], rows_in.at[0], halo_s.at[1], halo_r.at[0], below({})
+            px_hbm.at[pl.ds(tile_rows - REACH, REACH)], rows_in.at[0], halo_s.at[1], halo_r.at[0], below({})
         ),
         has_down,
     )
@@ -293,33 +307,29 @@
     for copy in own:
         copy.start()
 
-    bias[z] = jnp.broadcast_to(b_in[:, pl.ds(start, half)], (8, half))
-    for step in range(1, blks):
-        send(
-            lambda step=step: remote(
-                bias.at[z], bias.at[z], bias_s.at[step], bias_r.at[z], at_z((z + step) % blks)
-            )
-        )
-
     def body(i, _):
         pad[pl.ds(pl.multiple_of(i * 8 * wide, 8), 8 * wide), :] = jnp.zeros((8 * wide, 128), jnp.float32)
         return 0
 
-    lax.fori_loop(0, high, body, 0)
-    edge_f[...] = jnp.zeros_like(edge_f)
+    lax.fori_loop(0, 2 * high, body, 0)
+    for copy in loads:
+        copy.wait()
+
+    def spot_of(tile, line, col, group):
+        return ((tile * high + line) * wide + col) * GROUPS + group
 
     def put_row(values, group, line):
         for tile in range(2):
-            pad[pl.ds((line * wide + REACH) * 8 + 4 * tile + group, tile_cols, stride=8), :] = values[
+            pad[pl.ds(spot_of(tile, line, REACH, group), tile_cols, stride=GROUPS), :] = values[
                 :, tile * 128 : (tile + 1) * 128
             ]
 
-    for group in range(blks):
+    for group in range(GROUPS):
         low = REACH if group == 0 else 0
-        top = high - (REACH if group == blks - 1 else 0)
+        top = high - (REACH if group == GROUPS - 1 else 0)
 
         def body(line, _, group=group):
-            put_row(px[group * group_rows + line - REACH].astype(jnp.float32), group, line)
+            put_row(px[group * lines + line - REACH].astype(jnp.float32), group, line)
             return 0
 
         lax.fori_loop(low, top, body, 0)
@@ -327,10 +337,11 @@
     take = jnp.where(x == 0, tile_cols, REACH)
     for j in range(REACH):
         for tile in range(2):
-            for group in range(blks):
-                edge[j, group * group_rows : (group + 1) * group_rows, tile * 128 : (tile + 1) * 128] = pad[
-                    pl.ds((REACH * wide + take + j) * 8 + 4 * tile + group, group_rows, stride=8 * wide), :
-                ].astype(jnp.bfloat16)
+            for group in range(GROUPS):
+                edge_f[j, tile, group * lines : (group + 1) * lines, :] = pad[
+                    pl.ds(spot_of(tile, REACH, take + j, group), lines, stride=GROUPS * wide), :
+                ]
+            edge[j, :, tile * 128 : (tile + 1) * 128] = edge_f[j, tile, 0:tile_rows, :].astype(jnp.bfloat16)
     send(lambda: remote(edge, edge_in, halo_s.at[2], halo_r.at[2], side))
     send(
         lambda: remote(edge.at[:, pl.ds(0, 16)], corner_in.at[1], halo_s.at[3], halo_r.at[4], above(side)), has_up
@@ -342,18 +353,28 @@
         has_down,
     )
 
-    for i in range(KS):
-        for tile in range(2):
-            for group in range(4):
-                taps[pl.ds(i * KS * 8 + 4 * tile + group, KS, stride=8), :] = dwk[
-                    i, :, tile * 128 : (tile + 1) * 128
-                ]
-    upper = lax.broadcasted_iota(jnp.int32, (8, 128), 0) < 4
-
-    def tiled(ref):
-        return jnp.where(
-            upper, jnp.broadcast_to(ref[:, 0:128], (8, 128)), jnp.broadcast_to(ref[:, 128:256], (8, 128))
+    b_wide[...] = b_in[...].astype(jnp.float32)
+    share_rows = half // 128
+    for k in range(share_rows):
+        bias[z, :, k * 128 : (k + 1) * 128] = jnp.broadcast_to(b_wide[pl.ds(y * share_rows + k, 1), :], (8, 128))
+    for step in range(1, blks):
+        send(
+            lambda step=step: remote(
+                bias.at[z], bias.at[z], bias_s.at[step], bias_r.at[z], at_z((z + step) % blks)
+            )
         )
+    edge_f[...] = jnp.zeros_like(edge_f)
+
+    def spread(ref, tile):
+        return jnp.broadcast_to(ref[:, tile * 128 : (tile + 1) * 128], (GROUPS, 128))
+
+    for tile in range(2):
+        for i in range(KS):
+            for j in range(KS):
+                at = ((tile * KS + i) * KS + j) * GROUPS
+                taps[at : at + GROUPS, :] = jnp.broadcast_to(
+                    dwk[i, j : j + 1, tile * 128 : (tile + 1) * 128], (GROUPS, 128)
+                )
 
     @pl.when(has_up)
     def _():
@@ -365,7 +386,7 @@
     def _():
         arrived(rows_in.at[1], halo_s.at[1], halo_r.at[1], below({}))
         for i in range(REACH):
-            put_row(rows_in[1, i].astype(jnp.float32), blks - 1, high - REACH + i)
+            put_row(rows_in[1, i].astype(jnp.float32), GROUPS - 1, high - REACH + i)
 
     arrived(edge_in, halo_s.at[2], halo_r.at[2], side)
     for j in range(REACH):
@@ -395,46 +416,47 @@
     place = jnp.where(x == 0, tile_cols + REACH, 0)
     for j in range(REACH):
         for tile in range(2):
-            for group in range(blks):
-                pad[pl.ds((place + j) * 8 + 4 * tile + group, high, stride=8 * wide), :] = edge_f[
-                    j, tile, group * group_rows : group * group_rows + high, :
+            for group in range(GROUPS):
+                pad[pl.ds(spot_of(tile, 0, place + j, group), high, stride=GROUPS * wide), :] = edge_f[
+                    j, tile, group * lines : group * lines + high, :
                 ]
 
     def convolve(part):
-        def body(i, _):
-            line = part * part_rows + i // (tile_cols // 8)
-            col = (i % (tile_cols // 8)) * 8
-            total = jnp.broadcast_to(tiled(dw_bias)[None], (8, 8, 128))
-            for up in range(KS):
-                begin = pl.multiple_of(((line + up) * wide + col) * 8, 8)
-                cells = pad[pl.ds(begin, 8 * (7 + KS)), :].reshape(7 + KS, 8, 128)
-                for j in range(KS):
-                    weight = taps[(up * KS + j) * 8 : (up * KS + j + 1) * 8, :]
-                    total = total + cells[j : j + 8] * weight[None]
-            conv[pl.ds(pl.multiple_of((line * tile_cols + col) * 8, 64), 64), :] = total.reshape(64, 128)
-            return 0
-
-        lax.fori_loop(0, part_px // 8, body, 0)
-
-    def both_tiles(values):
-        return values + pltpu.roll(values, 4, 1)
+        for tile in range(2):
+
+            def body(i, _, tile=tile):
+                line = part * part_rows + i // (tile_cols // 8)
+                col = (i % (tile_cols // 8)) * 8
+                total = jnp.broadcast_to(spread(dw_bias, tile)[None], (8, GROUPS, 128))
+                for up in range(KS):
+                    begin = pl.multiple_of(spot_of(tile, line + up, col, 0), 8)
+                    cells = pad[pl.ds(begin, GROUPS * (7 + KS)), :].reshape(7 + KS, GROUPS, 128)
+                    for j in range(KS):
+                        at = ((tile * KS + up) * KS + j) * GROUPS
+                        total = total + cells[j : j + 8] * taps[at : at + GROUPS, :][None]
+                begin = pl.multiple_of((line * tile_cols + col) * GROUPS, 64)
+                conv[tile, pl.ds(begin, 8 * GROUPS), :] = total.reshape(8 * GROUPS, 128)
+                return 0
+
+            lax.fori_loop(0, group_px // 8, body, 0)
+
+    def cells_of(part, b):
+        where = pl.ds(pl.multiple_of(part * part_regs + b * BLOCK, BLOCK), BLOCK)
+        return where, [conv[tile, where, :].reshape(BLOCK // 8, 8, 128) for tile in range(2)]
 
     def measure(part):
         def body(b, _):
-            cells = conv[pl.ds(pl.multiple_of(part * part_regs + b * BLOCK, BLOCK), BLOCK), :].reshape(
-                BLOCK // 8, 8, 128
-            )
-            sums = jnp.broadcast_to(jnp.sum(cells, axis=2, keepdims=True), cells.shape)
-            mean = both_tiles(sums) * (1.0 / chans)
-            off = cells - mean
-            squares = both_tiles(jnp.broadcast_to(jnp.sum(off * off, axis=2, keepdims=True), cells.shape))
-            lane = lax.broadcasted_iota(jnp.int32, cells.shape, 2)
+            _, cells = cells_of(part, b)
+            mean = jnp.sum(cells[0] + cells[1], axis=2, keepdims=True) * (1.0 / chans)
+            off = [values - mean for values in cells]
+            squares = jnp.sum(off[0] * off[0] + off[1] * off[1], axis=2, keepdims=True)
+            lane = lax.broadcasted_iota(jnp.int32, cells[0].shape, 2)
             turned = jnp.where(lane == 0, mean, squares).reshape(BLOCK, 128).T
-            stat[part, z, 0, pl.ds(b, 1), :] = turned[0:1]
-            stat[part, z, 1, pl.ds(b, 1), :] = turned[1:2]
+            stat[part, z, pl.ds(b, 1), :] = turned[0:1]
+            stat[part, z, pl.ds(STATS + b, 1), :] = turned[1:2]
             return 0
 
-        lax.fori_loop(0, stat_blocks, body, 0)
+        lax.fori_loop(0, STATS, body, 0)
         for step in range(1, blks):
             send(
                 lambda step=step: remote(
@@ -450,27 +472,30 @@
         for step in range(1, blks):
             other = (z + step) % blks
             arrived(stat.at[part, other], stat_s.at[part, step], stat_r.at[part, other], at_z(other))
-        mean = sum(stat[part, o, 0] for o in range(blks)) / blks
-        spread = sum(stat[part, o, 1] + chans * (stat[part, o, 0] - mean) ** 2 for o in range(blks)) / full
+        mean = sum(stat[part, o, 0:STATS] for o in range(blks)) / blks
+        spread_sum = sum(
+            stat[part, o, STATS : 2 * STATS] + chans * (stat[part, o, 0:STATS] - mean) ** 2 for o in range(blks)
+        )
         norm_stat[0] = mean
-        norm_stat[1] = lax.rsqrt(spread + 1e-06)
+        norm_stat[1] = lax.rsqrt(spread_sum / full + 1e-06)
 
         def body(b, _):
-            where = pl.ds(pl.multiple_of(part * part_regs + b * BLOCK, BLOCK), BLOCK)
-            cells = conv[where, :].reshape(BLOCK // 8, 8, 128)
+            where, cells = cells_of(part, b)
             means, scales = (
                 jnp.broadcast_to(norm_stat[k, pl.ds(b, 1), :], (BLOCK, 128)).T.reshape(BLOCK // 8, 8, 128)
                 for k in range(2)
             )
-            normed = (cells - means) * scales * tiled(gain)[None] + tiled(beta)[None]
-            conv[where, :] = normed.reshape(BLOCK, 128)
+            for tile in range(2):
+                normed = (cells[tile] - means) * scales * spread(gain, tile)[None] + spread(beta, tile)[None]
+                conv[tile, where, :] = normed.reshape(BLOCK, 128)
             return 0
 
-        lax.fori_loop(0, stat_blocks, body, 0)
-        for group in range(blks):
+        lax.fori_loop(0, STATS, body, 0)
+        for group in range(GROUPS):
+            begin = (group % per_blk) * group_px
             for tile in range(2):
-                a_send[part, group, :, tile * 128 : (tile + 1) * 128] = conv[
-                    pl.ds(part * part_regs + 4 * tile + group, part_px, stride=8), :
+                a_send[part, group // per_blk, begin : begin + group_px, tile * 128 : (tile + 1) * 128] = conv[
+                    tile, pl.ds(part * part_regs + group, group_px, stride=GROUPS), :
                 ].astype(jnp.bfloat16)
         for step in range(1, blks):
             send(
@@ -482,22 +507,28 @@
         pltpu.make_async_copy(
             a_send.at[part, z], act.at[part, pl.ds(0, part_px), columns(z)], a_l.at[part]
         ).start()
+        send(
+            lambda: remote(
+                a_send.at[part, z], act.at[part, pl.ds(part_px, part_px), columns(z)],
+                y_s.at[part, 0], y_r.at[part, z], partner,
+            )
+        )
 
     def swap_rows(part):
-        for step in range(1, blks):
+        for step in (1, 3, 2):
             other = (z + step) % blks
-            arrived(
-                act.at[part, pl.ds(0, part_px), columns(other)], a_s.at[part, step], a_r.at[part, other], at_z(other)
+            held = act.at[part, pl.ds(0, part_px), columns(other)]
+            arrived(held, a_s.at[part, step], a_r.at[part, other], at_z(other))
+            send(
+                lambda other=other, step=step: remote(
+                    act.at[part, pl.ds(0, part_px), columns(other)],
+                    act.at[part, pl.ds(part_px, part_px), columns(other)],
+                    y_s.at[part, step], y_r.at[part, other], partner,
+                )
             )
         pltpu.make_async_copy(
             a_send.at[part, z], act.at[part, pl.ds(0, part_px), columns(z)], a_l.at[part]
         ).wait()
-        send(
-            lambda: remote(
-                act.at[part, pl.ds(0, part_px)], act.at[part, pl.ds(part_px, part_px)],
-                y_s.at[part], y_r.at[part], partner,
-            )
-        )
 
     def both_ways(dist):
         return ((z >= dist, lambda: z - dist, z < blks - 1, 1), (z + dist < blks, lambda: z + dist, z > 0, -1))
@@ -562,7 +593,11 @@
                     )
 
     def feed(part):
-        arrived(act.at[part, pl.ds(part_px, part_px)], y_s.at[part], y_r.at[part], partner)
+        for step in range(blks):
+            other = (z + step) % blks
+            arrived(
+                act.at[part, pl.ds(part_px, part_px), columns(other)], y_s.at[part, step], y_r.at[part, other], partner
+            )
 
         def body(o, _):
             pre_act = lax.dot_general(
@@ -583,29 +618,45 @@
             return 0
 
         lax.fori_loop(0, blks, body, 0)
-        p_send[part] = acc[part, part_px:, :].astype(jnp.bfloat16)
-        send(lambda: remote(p_send.at[part], p_in.at[part], p_s.at[part], p_r.at[part], partner))
-
-    def result_rows(owner, part):
-        return out.at[pl.ds(pl.multiple_of(owner * (part_px * PARTS) + part * part_px, part_px), part_px)]
+        for n in range(per_blk):
+            rows = slice(n * group_px, (n + 1) * group_px)
+            p_send[part, rows, :] = acc[part, part_px + n * group_px : part_px + (n + 1) * group_px, :].astype(
+                jnp.bfloat16
+            )
+            send(
+                lambda n=n: remote(
+                    p_send.at[part, pl.ds(n * group_px, group_px)], p_in.at[part, pl.ds(n * group_px, group_px)],
+                    p_s.at[part, n], p_r.at[part, n], partner,
+                )
+            )
+
+    def result_rows(owner, part, n):
+        begin = owner * (per_blk * lines * tile_cols) + n * (lines * tile_cols) + part * group_px
+        return out.at[pl.ds(pl.multiple_of(begin, group_px), group_px)]
+
+    def sums_for(owner, part, n):
+        return r_send.at[part, pl.ds(n * group_px, group_px), columns(owner)]
 
     def give_back(part):
-        arrived(p_in.at[part], p_s.at[part], p_r.at[part], partner)
-        r_send[part] = (acc[part, :part_px, :] + p_in[part].astype(jnp.float32)).astype(jnp.bfloat16)
-        for step in range(1, blks):
-            send(
-                lambda step=step: remote(
-                    r_send.at[part, :, columns((z + step) % blks)], result_rows(z, part),
-                    r_s.at[part, step], r_r.at[part, z], at_z((z + step) % blks),
+        for n in range(per_blk):
+            rows = slice(n * group_px, (n + 1) * group_px)
+            arrived(p_in.at[part, pl.ds(n * group_px, group_px)], p_s.at[part, n], p_r.at[part, n], partner)
+            r_send[part, rows, :] = (acc[part, rows, :] + p_in[part, rows, :].astype(jnp.float32)).astype(jnp.bfloat16)
+            for step in range(1, blks):
+                send(
+                    lambda step=step, n=n: remote(
+                        sums_for((z + step) % blks, part, n), result_rows(z, part, n),
+                        r_s.at[part, n, step], r_r.at[part, n, z], at_z((z + step) % blks),
+                    )
                 )
-            )
-        pltpu.make_async_copy(r_send.at[part, :, columns(z)], result_rows(z, part), r_l.at[part]).start()
+            pltpu.make_async_copy(sums_for(z, part, n), result_rows(z, part, n), r_l.at[part, n]).start()
 
     def collect(part):
-        for step in range(1, blks):
-            other = (z + step) % blks
-            arrived(result_rows(other, part), r_s.at[part, step], r_r.at[part, other], at_z(other))
-        pltpu.make_async_copy(r_send.at[part, :, columns(z)], result_rows(z, part), r_l.at[part]).wait()
+        for n in range(per_blk):
+            for step in range(1, blks):
+                other = (z + step) % blks
+                arrived(result_rows(other, part, n), r_s.at[part, n, step], r_r.at[part, n, other], at_z(other))
+            pltpu.make_async_copy(sums_for(z, part, n), result_rows(z, part, n), r_l.at[part, n]).wait()
 
     convolve(0)
     measure(0)
@@ -623,17 +674,17 @@
     convolve(3)
     measure(3)
     normalize(2)
+    relay(2, 1)
     normalize(3)
-    relay(2, 1)
     share(2, 0)
-    swap_rows(0)
     relay(3, 0)
     share(2, 1)
-    swap_rows(1)
     relay(3, 1)
     share(3, 0)
+    swap_rows(0)
+    swap_rows(1)
+    share(3, 1)
     swap_rows(2)
-    share(3, 1)
     ready()
     feed(0)
     swap_rows(3)
@@ -654,31 +705,39 @@
     tile_rows, tile_cols, chans = pixels.shape
     blks = lax.axis_size("blk")
     full = blks * chans
-    half = w_in.shape[0] // 2
-    group_rows = tile_rows // blks
-    px = group_rows * tile_cols
-    part_px = px // PARTS
-    high, wide = group_rows + 2 * REACH, tile_cols + 2 * REACH
+    hidden = w_in.shape[0]
+    half = hidden // 2
+    lines = tile_rows // GROUPS
+    part_px = tile_rows * tile_cols // (blks * PARTS)
+    pairs = GROUPS // blks
+    high, wide = lines + 2 * REACH, tile_cols + 2 * REACH
     vmem, dma = pltpu.VMEM, pltpu.SemaphoreType.DMA
-    here = pl.BlockSpec(memory_space=pltpu.VMEM)
     anywhere = pl.BlockSpec(memory_space=pl.ANY)
     bf16, f32 = jnp.bfloat16, jnp.float32
     summed = pl.pallas_call(
         fused_kernel,
-        in_specs=[here] * 6 + [anywhere] * 2,
+        in_specs=[pl.BlockSpec(memory_space=pltpu.HBM)] * 8,
         out_specs=anywhere,
         out_shape=jax.ShapeDtypeStruct((tile_rows * tile_cols, chans), bf16),
         scratch_shapes=[
-            vmem((high * wide * 8, 128), f32),
-            vmem((KS * KS * 8, 128), f32),
-            vmem((px * 8, 128), f32),
+            vmem(pixels.shape, bf16),
+            vmem(dw_kernel.shape, f32),
+            vmem((1, chans), f32),
+            vmem((1, chans), f32),
+            vmem((1, chans), f32),
+            vmem((hidden // 128, 128), bf16),
+            vmem((hidden // 128, 128), f32),
+            dma((6,)),
+            vmem((2 * high * wide * GROUPS, 128), f32),
+            vmem((2 * KS * KS * GROUPS, 128), f32),
+            vmem((2, lines * tile_cols * GROUPS, 128), f32),
             vmem((REACH, tile_rows, chans), bf16),
             vmem((REACH, tile_rows, chans), bf16),
             vmem((2, REACH, tile_cols, chans), bf16),
             vmem((2, REACH, 16, chans), bf16),
             vmem((REACH, 2, tile_rows + 8, 128), f32),
-            vmem((PARTS, blks, 2, 8, 128), f32),
-            vmem((2, 8, 128), f32),
+            vmem((PARTS, blks, 2 * STATS, 128), f32),
+            vmem((2, STATS, 128), f32),
             vmem((blks, 8, half), f32),
             vmem((blks, half, full), bf16),
             vmem((blks, half, full), bf16),
@@ -692,15 +751,15 @@
             dma((2, 2)), dma((2, blks)), dma((2, blks)), dma((2, blks)), dma((2, blks)),
             dma((2, 2, blks)), dma((2, 2, blks)),
             dma((PARTS, blks)), dma((PARTS, blks)), dma((PARTS,)),
-            dma((PARTS,)), dma((PARTS,)), dma((PARTS,)), dma((PARTS,)),
-            dma((PARTS, blks)), dma((PARTS, blks)), dma((PARTS,)),
+            dma((PARTS, blks)), dma((PARTS, blks)), dma((PARTS, pairs)), dma((PARTS, pairs)),
+            dma((PARTS, pairs, blks)), dma((PARTS, pairs, blks)), dma((PARTS, pairs)),
         ],
         compiler_params=pltpu.CompilerParams(
-            collective_id=0, has_side_effects=True, vmem_limit_bytes=48 * 1024 * 1024
+            collective_id=0, has_side_effects=True, vmem_limit_bytes=64 * 1024 * 1024
         ),
     )(
         pixels, dw_kernel, dw_bias[None, :], ln_gain[None, :], ln_bias[None, :],
-        b_in.astype(f32)[None, :], w_in, w_out,
+        b_in.reshape(hidden // 128, 128), w_in, w_out,
     )
     result = pixels.astype(f32) + layer_scale * (
         summed.astype(f32).reshape(tile_rows, tile_cols, chans) + b_out
@@ -713,9 +772,7 @@
     blks = lax.axis_size("blk")
     fits = (
         (lax.axis_size("y"), lax.axis_size("col"), blks, chans) == (2, 2, 4, 256)
-        and tile_cols % 16 == 0
-        and tile_rows % (4 * blks) == 0
-        and tile_rows * tile_cols == blks * PARTS * BLOCK
+        and (tile_rows, tile_cols) == (64, 32)
         and params[4].shape[0] % 1024 == 0
     )
     return (fused if fits else general)(pixels, *params)

time: 118 us -> 109 us (0.924)
  local copies, waits for them, and re-layouts: 5.68 us -> 0 us
  Pallas kernels: 110 us -> 106 us
    unnamed x16 -> x0, local copies, waits for them, and re-layouts: 5.68 us -> none
    pallas_call x1, Pallas kernels: 110 us -> 106 us  [fused(): pl.pallas_call(fused_kernel, in_specs=[pl.BlockSpec(memory_space=pltpu.HB...]
    convert_element_type x1, other arithmetic: 1.42 us -> 2.95 us  [fused(): return result.astype(bf16)]
where the time goes in v2:
time: 109 us
  Pallas kernels  106 us (97%)
  other arithmetic  2.95 us (3%)
    pallas_call x1, Pallas kernels, fused(): pl.pallas_call(fused_kernel, in_specs=[pl.BlockSpec(memory_space=pltpu.HB...  106 us
    convert_element_type x1, other arithmetic, fused(): return result.astype(bf16)  2.95 us

profile of v2, /device:TPU:0, one launch (start us, length us, event | category | flops | bytes accessed | tf_op | source)
XLA Modules:
  0.0 109.4 jit_solution(10423776404154707029)
XLA Ops:
  0.0 106.4 %shard_map.100 = bf16[2048,256]{1,0:T(8,128)(2,1)} custom-call(bf16[64,32,256]{2,1,0:T(8,128)(2,1)} %px_hbm.1, f32[7,7,256]{2,1,0:T(8,128)} %dwk_hbm.1, f32[1,256]{1,0:T(1,128)} %bitcast.8, f32[1,256]{1,0:T(1,128)} %bitcast.9, f32[1,256]{1,0:T(1,128)} %bitcast.10, bf16[8,128]{1,0:T(8,128)(2,1)} %bitcast.7, bf16[1024,1024]{1,0:T(8,128)(2,1)} %w_in.1, ...), custom_call_target="tpu_custom_call" | custom-call | tf_op jit(solution)/shard_map/pallas_call | solution.py:717
  106.4 3.0 %fusion.2 = bf16[64,32,256]{2,1,0:T(8,128)(2,1)} fusion(bf16[64,32,256]{2,1,0:T(8,128)(2,1)} %bitcast.6, bf16[64,32,256]{2,1,0:T(8,128)(2,1)} %px_hbm.1, f32[256]{0:T(256)} %param.18, f32[256]{0:T(256)} %param.19), kind=kLoop, calls=%fused_computation.3 | loop fusion | flops 3145728 | bytes 3147776 | tf_op jit(solution)/shard_map/convert_element_type | solution.py:767

commit v3 on v2

--- a/solution.py
+++ b/solution.py
@@ -189,7 +189,7 @@
 def fused_kernel(
     px_hbm, dwk_hbm, dw_bias_hbm, gain_hbm, beta_hbm, b_in_hbm, w_in, w_out,
     out,
-    px, dwk, dw_bias, gain, beta, b_in, b_wide, load_sem,
+    px, dwk, dw_bias, gain, beta, b_in, b_all, load_sem,
     pad, taps, conv, edge, edge_in, rows_in, corner_in, edge_f, stat, norm_stat, bias,
     first, second, a_send, act, acc, p_send, p_in, r_send,
     own_sem, halo_s, halo_r, bias_s, bias_r, stat_s, stat_r,
@@ -203,8 +203,8 @@
     row = 2 * y + c
     lines = tile_rows // GROUPS
     high, wide = lines + 2 * REACH, tile_cols + 2 * REACH
-    half = first.shape[1]
-    eighth = half // 4
+    quarter = first.shape[2]
+    eighth = quarter // 2
     per_blk = GROUPS // blks
     part_rows = lines // PARTS
     group_px = part_rows * tile_cols
@@ -287,22 +287,38 @@
         has_down,
     )
 
-    start = pl.multiple_of(y * half, half)
-    mine = pl.multiple_of(x * (half // 2) + c * eighth, eighth)
-    across = pl.multiple_of((1 - x) * (half // 2) + c * eighth, eighth)
+    quarters = (2 * y + x, 2 * y + 1 - x, 2 * (1 - y) + x)
+    mine = pl.ds(pl.multiple_of(c * eighth, eighth), eighth)
+    theirs = pl.ds(pl.multiple_of((1 - c) * eighth, eighth), eighth)
+    start = pl.multiple_of(quarters[0] * quarter + c * eighth, eighth)
     weights = ((w_in, first), (w_out, second))
-    for k, (src, dst) in enumerate(weights):
-        piece = lambda src=src: src.at[pl.ds(pl.multiple_of(start + mine, eighth), eighth)]
+
+    def mate(part):
+        return partner if part % 2 == 0 else side
+
+    def own_copies(k):
+        src, dst = weights[k]
         for way, cond, step in ((0, z < blks - 1, 1), (1, z > 0, -1)):
-            send(
-                lambda k=k, way=way, step=step, piece=piece, dst=dst: remote(
-                    piece(), dst.at[z, pl.ds(mine, eighth)], zown_s.at[k, way], z_r.at[k, z], at_z(z + step)
-                ),
-                cond,
-            )
+            yield cond, lambda way=way, step=step: remote(
+                src.at[pl.ds(start, eighth)], dst.at[z, 0, mine],
+                zown_s.at[k, way], z_r.at[k, z], at_z(z + step),
+            )
+
+    def own_out(k):
+        for cond, make in own_copies(k):
+            when(cond, lambda make=make: make().start())
+
+    def own_gone(k):
+        for cond, make in own_copies(k):
+            when(cond, lambda make=make: make().wait_send())
+
+    own_out(0)
     own = [
-        pltpu.make_async_copy(src.at[pl.ds(start, half)], dst.at[z], own_sem.at[k])
+        pltpu.make_async_copy(
+            src.at[pl.ds(pl.multiple_of(quarters[n] * quarter, quarter), quarter)], dst.at[z, n], own_sem.at[k, n]
+        )
         for k, (src, dst) in enumerate(weights)
+        for n in range(3)
     ]
     for copy in own:
         copy.start()
@@ -353,14 +369,11 @@
         has_down,
     )
 
-    b_wide[...] = b_in[...].astype(jnp.float32)
-    share_rows = half // 128
-    for k in range(share_rows):
-        bias[z, :, k * 128 : (k + 1) * 128] = jnp.broadcast_to(b_wide[pl.ds(y * share_rows + k, 1), :], (8, 128))
+    b_all[z] = b_in[...].astype(jnp.float32)
     for step in range(1, blks):
         send(
             lambda step=step: remote(
-                bias.at[z], bias.at[z], bias_s.at[step], bias_r.at[z], at_z((z + step) % blks)
+                b_all.at[z], b_all.at[z], bias_s.at[step], bias_r.at[z], at_z((z + step) % blks)
             )
         )
     edge_f[...] = jnp.zeros_like(edge_f)
@@ -376,50 +389,51 @@
                     dwk[i, j : j + 1, tile * 128 : (tile + 1) * 128], (GROUPS, 128)
                 )
 
-    @pl.when(has_up)
-    def _():
-        arrived(rows_in.at[0], halo_s.at[0], halo_r.at[0], above({}))
-        for i in range(REACH):
-            put_row(rows_in[0, i].astype(jnp.float32), 0, i)
-
-    @pl.when(has_down)
-    def _():
-        arrived(rows_in.at[1], halo_s.at[1], halo_r.at[1], below({}))
-        for i in range(REACH):
-            put_row(rows_in[1, i].astype(jnp.float32), GROUPS - 1, high - REACH + i)
-
-    arrived(edge_in, halo_s.at[2], halo_r.at[2], side)
-    for j in range(REACH):
-        for tile in range(2):
-            edge_f[j, tile, REACH : REACH + tile_rows, :] = edge_in[
-                j, :, tile * 128 : (tile + 1) * 128
-            ].astype(jnp.float32)
-
-    @pl.when(has_up)
-    def _():
-        arrived(corner_in.at[0], halo_s.at[3], halo_r.at[3], above(side))
+    def finish_halo():
+        @pl.when(has_up)
+        def _():
+            arrived(rows_in.at[0], halo_s.at[0], halo_r.at[0], above({}))
+            for i in range(REACH):
+                put_row(rows_in[0, i].astype(jnp.float32), 0, i)
+
+        @pl.when(has_down)
+        def _():
+            arrived(rows_in.at[1], halo_s.at[1], halo_r.at[1], below({}))
+            for i in range(REACH):
+                put_row(rows_in[1, i].astype(jnp.float32), GROUPS - 1, high - REACH + i)
+
+        arrived(edge_in, halo_s.at[2], halo_r.at[2], side)
         for j in range(REACH):
             for tile in range(2):
-                edge_f[j, tile, 0:REACH, :] = corner_in[0, j, :, tile * 128 : (tile + 1) * 128].astype(
-                    jnp.float32
-                )[16 - REACH :]
-
-    @pl.when(has_down)
-    def _():
-        arrived(corner_in.at[1], halo_s.at[4], halo_r.at[4], below(side))
+                edge_f[j, tile, REACH : REACH + tile_rows, :] = edge_in[
+                    j, :, tile * 128 : (tile + 1) * 128
+                ].astype(jnp.float32)
+
+        @pl.when(has_up)
+        def _():
+            arrived(corner_in.at[0], halo_s.at[3], halo_r.at[3], above(side))
+            for j in range(REACH):
+                for tile in range(2):
+                    edge_f[j, tile, 0:REACH, :] = corner_in[0, j, :, tile * 128 : (tile + 1) * 128].astype(
+                        jnp.float32
+                    )[16 - REACH :]
+
+        @pl.when(has_down)
+        def _():
+            arrived(corner_in.at[1], halo_s.at[4], halo_r.at[4], below(side))
+            for j in range(REACH):
+                for tile in range(2):
+                    edge_f[j, tile, REACH + tile_rows : 2 * REACH + tile_rows, :] = corner_in[
+                        1, j, :, tile * 128 : (tile + 1) * 128
+                    ].astype(jnp.float32)[:REACH]
+
+        place = jnp.where(x == 0, tile_cols + REACH, 0)
         for j in range(REACH):
             for tile in range(2):
-                edge_f[j, tile, REACH + tile_rows : 2 * REACH + tile_rows, :] = corner_in[
-                    1, j, :, tile * 128 : (tile + 1) * 128
-                ].astype(jnp.float32)[:REACH]
-
-    place = jnp.where(x == 0, tile_cols + REACH, 0)
-    for j in range(REACH):
-        for tile in range(2):
-            for group in range(GROUPS):
-                pad[pl.ds(spot_of(tile, 0, place + j, group), high, stride=GROUPS * wide), :] = edge_f[
-                    j, tile, group * lines : group * lines + high, :
-                ]
+                for group in range(GROUPS):
+                    pad[pl.ds(spot_of(tile, 0, place + j, group), high, stride=GROUPS * wide), :] = edge_f[
+                        j, tile, group * lines : group * lines + high, :
+                    ]
 
     def convolve(part):
         for tile in range(2):
@@ -497,22 +511,24 @@
                 a_send[part, group // per_blk, begin : begin + group_px, tile * 128 : (tile + 1) * 128] = conv[
                     tile, pl.ds(part * part_regs + group, group_px, stride=GROUPS), :
                 ].astype(jnp.bfloat16)
-        for step in range(1, blks):
-            send(
-                lambda step=step: remote(
-                    a_send.at[part, (z + step) % blks], act.at[part, pl.ds(0, part_px), columns(z)],
-                    a_s.at[part, step], a_r.at[part, z], at_z((z + step) % blks),
-                )
-            )
         pltpu.make_async_copy(
             a_send.at[part, z], act.at[part, pl.ds(0, part_px), columns(z)], a_l.at[part]
         ).start()
         send(
             lambda: remote(
                 a_send.at[part, z], act.at[part, pl.ds(part_px, part_px), columns(z)],
-                y_s.at[part, 0], y_r.at[part, z], partner,
+                y_s.at[part, 0], y_r.at[part, z], mate(part),
             )
         )
+
+    def regroup(part):
+        for step in (2, 1, 3):
+            send(
+                lambda step=step: remote(
+                    a_send.at[part, (z + step) % blks], act.at[part, pl.ds(0, part_px), columns(z)],
+                    a_s.at[part, step], a_r.at[part, z], at_z((z + step) % blks),
+                )
+            )
 
     def swap_rows(part):
         for step in (1, 3, 2):
@@ -523,7 +539,7 @@
                 lambda other=other, step=step: remote(
                     act.at[part, pl.ds(0, part_px), columns(other)],
                     act.at[part, pl.ds(part_px, part_px), columns(other)],
-                    y_s.at[part, step], y_r.at[part, other], partner,
+                    y_s.at[part, step], y_r.at[part, other], mate(part),
                 )
             )
         pltpu.make_async_copy(
@@ -533,27 +549,38 @@
     def both_ways(dist):
         return ((z >= dist, lambda: z - dist, z < blks - 1, 1), (z + dist < blks, lambda: z + dist, z > 0, -1))
 
-    def relay(dist, k):
+    def passed_on(dist, k):
         block = weights[k][1]
         for cond, origin, more, step in both_ways(dist):
-            spot = lambda origin=origin: block.at[origin(), pl.ds(mine, eighth)]
+            spot = lambda origin=origin: block.at[origin(), 0, mine]
+            yield cond & more, lambda spot=spot, origin=origin, step=step: remote(
+                spot(), spot(), zfwd_s.at[k, origin()], z_r.at[k, origin()], at_z(z + step)
+            )
+
+    def forward(dist, k):
+        for cond, make in passed_on(dist, k):
+            when(cond, lambda make=make: make().start())
+
+    def forwarded(dist, k):
+        for cond, make in passed_on(dist, k):
+            when(cond, lambda make=make: make().wait_send())
+
+    def take_in(dist, k):
+        block = weights[k][1]
+        for cond, origin, _, _ in both_ways(dist):
+            spot = lambda origin=origin: block.at[origin(), 0, mine]
             when(
                 cond,
                 lambda spot=spot, origin=origin: arrived(spot(), zown_s.at[k, 0], z_r.at[k, origin()], side),
             )
-            if dist < blks - 1:
+            for n, device in ((1, side), (2, partner)):
                 send(
-                    lambda spot=spot, origin=origin, step=step: remote(
-                        spot(), spot(), zfwd_s.at[k, origin()], z_r.at[k, origin()], at_z(z + step)
+                    lambda spot=spot, origin=origin, n=n, device=device: remote(
+                        spot(), block.at[origin(), n, mine], x_s.at[k, n - 1, origin()], x_r.at[k, n - 1, origin()],
+                        device,
                     ),
-                    cond & more,
+                    cond,
                 )
-            send(
-                lambda spot=spot, origin=origin: remote(
-                    spot(), spot(), x_s.at[k, origin()], x_r.at[k, origin()], side
-                ),
-                cond,
-            )
             send(
                 lambda spot=spot, origin=origin: remote(
                     spot(), spot(), c_s.at[k, 0, origin()], c_r.at[k, 0, origin()], sibling
@@ -564,48 +591,57 @@
     def share(dist, k):
         block = weights[k][1]
         for cond, origin, _, _ in both_ways(dist):
-            spot = lambda origin=origin: block.at[origin(), pl.ds(across, eighth)]
-            when(
-                cond,
-                lambda spot=spot, origin=origin: arrived(
-                    spot(), x_s.at[k, origin()], x_r.at[k, origin()], side
-                ),
-            )
-            send(
-                lambda spot=spot, origin=origin: remote(
-                    spot(), spot(), c_s.at[k, 1, origin()], c_r.at[k, 1, origin()], sibling
-                ),
-                cond,
-            )
+            for n, device in ((1, side), (2, partner)):
+                spot = lambda origin=origin, n=n: block.at[origin(), n, mine]
+                when(
+                    cond,
+                    lambda spot=spot, origin=origin, n=n, device=device: arrived(
+                        spot(), x_s.at[k, n - 1, origin()], x_r.at[k, n - 1, origin()], device
+                    ),
+                )
+                send(
+                    lambda spot=spot, origin=origin, n=n: remote(
+                        spot(), spot(), c_s.at[k, n, origin()], c_r.at[k, n, origin()], sibling
+                    ),
+                    cond,
+                )
 
     def ready():
         for copy in own:
             copy.wait()
         for step in range(1, blks):
             other = (z + step) % blks
-            arrived(bias.at[other], bias_s.at[step], bias_r.at[other], at_z(other))
+            arrived(b_all.at[other], bias_s.at[step], bias_r.at[other], at_z(other))
             for k in range(2):
-                for n, column in ((0, x), (1, 1 - x)):
-                    begin = pl.multiple_of(column * (half // 2) + (1 - c) * eighth, eighth)
-                    arrived(
-                        weights[k][1].at[other, pl.ds(begin, eighth)],
-                        c_s.at[k, n, other], c_r.at[k, n, other], sibling,
+                for n in range(3):
+                    arrived(weights[k][1].at[other, n, theirs], c_s.at[k, n, other], c_r.at[k, n, other], sibling)
+        wide_rows = quarter // 128
+        for o in range(blks):
+            for n in range(3):
+                for k in range(wide_rows):
+                    bias[o, n, :, k * 128 : (k + 1) * 128] = jnp.broadcast_to(
+                        b_all[o, pl.ds(quarters[n] * wide_rows + k, 1), :], (8, 128)
                     )
 
     def feed(part):
         for step in range(blks):
             other = (z + step) % blks
             arrived(
-                act.at[part, pl.ds(part_px, part_px), columns(other)], y_s.at[part, step], y_r.at[part, other], partner
-            )
+                act.at[part, pl.ds(part_px, part_px), columns(other)], y_s.at[part, step], y_r.at[part, other], mate(part)
+            )
+
+        def hidden_of(o, n):
+            pre_act = lax.dot_general(
+                act[part], first[o, n], (((1,), (1,)), ((), ())), preferred_element_type=jnp.float32
+            )
+            pre_act = pre_act + bias[o, n, 0:1, :]
+            return (0.5 * pre_act * (1.0 + lax.erf(pre_act * 0.7071067811865476))).astype(jnp.bfloat16)
 
         def body(o, _):
-            pre_act = lax.dot_general(
-                act[part], first[o], (((1,), (1,)), ((), ())), preferred_element_type=jnp.float32
-            )
-            pre_act = pre_act + bias[o, 0:1, :]
-            hidden = 0.5 * pre_act * (1.0 + lax.erf(pre_act * 0.7071067811865476))
-            term = jnp.dot(hidden.astype(jnp.bfloat16), second[o], preferred_element_type=jnp.float32)
+            term = sum(
+                jnp.dot(hidden_of(o, n), second[o, n], preferred_element_type=jnp.float32)
+                for n in (0, 1 + part % 2)
+            )
 
             @pl.when(o == 0)
             def _():
@@ -626,7 +662,7 @@
             send(
                 lambda n=n: remote(
                     p_send.at[part, pl.ds(n * group_px, group_px)], p_in.at[part, pl.ds(n * group_px, group_px)],
-                    p_s.at[part, n], p_r.at[part, n], partner,
+                    p_s.at[part, n], p_r.at[part, n], mate(part),
                 )
             )
 
@@ -640,7 +676,7 @@
     def give_back(part):
         for n in range(per_blk):
             rows = slice(n * group_px, (n + 1) * group_px)
-            arrived(p_in.at[part, pl.ds(n * group_px, group_px)], p_s.at[part, n], p_r.at[part, n], partner)
+            arrived(p_in.at[part, pl.ds(n * group_px, group_px)], p_s.at[part, n], p_r.at[part, n], mate(part))
             r_send[part, rows, :] = (acc[part, rows, :] + p_in[part, rows, :].astype(jnp.float32)).astype(jnp.bfloat16)
             for step in range(1, blks):
                 send(
@@ -658,33 +694,49 @@
                 arrived(result_rows(other, part, n), r_s.at[part, n, step], r_r.at[part, n, other], at_z(other))
             pltpu.make_async_copy(sums_for(z, part, n), result_rows(z, part, n), r_l.at[part, n]).wait()
 
+    own_gone(0)
+    own_out(1)
+    take_in(1, 0)
+    finish_halo()
     convolve(0)
     measure(0)
-    relay(1, 0)
+    own_gone(1)
+    forward(1, 0)
+    take_in(1, 1)
     convolve(1)
     measure(1)
     normalize(0)
-    relay(1, 1)
+    forwarded(1, 0)
+    forward(1, 1)
+    take_in(2, 0)
     share(1, 0)
     convolve(2)
     measure(2)
     normalize(1)
-    relay(2, 0)
+    forwarded(1, 1)
+    forward(2, 0)
+    take_in(2, 1)
+    regroup(0)
     share(1, 1)
     convolve(3)
     measure(3)
     normalize(2)
-    relay(2, 1)
+    forwarded(2, 0)
+    forward(2, 1)
+    take_in(3, 0)
+    share(2, 0)
     normalize(3)
-    share(2, 0)
-    relay(3, 0)
+    swap_rows(0)
+    regroup(1)
+    forwarded(2, 1)
+    take_in(3, 1)
     share(2, 1)
-    relay(3, 1)
     share(3, 0)
-    swap_rows(0)
     swap_rows(1)
+    regroup(2)
     share(3, 1)
     swap_rows(2)
+    regroup(3)
     ready()
     feed(0)
     swap_rows(3)
@@ -706,7 +758,6 @@
     blks = lax.axis_size("blk")
     full = blks * chans
     hidden = w_in.shape[0]
-    half = hidden // 2
     lines = tile_rows // GROUPS
     part_px = tile_rows * tile_cols // (blks * PARTS)
     pairs = GROUPS // blks
@@ -726,7 +777,7 @@
             vmem((1, chans), f32),
             vmem((1, chans), f32),
             vmem((hidden // 128, 128), bf16),
-            vmem((hidden // 128, 128), f32),
+            vmem((blks, hidden // 128, 128), f32),
             dma((6,)),
             vmem((2 * high * wide * GROUPS, 128), f32),
             vmem((2 * KS * KS * GROUPS, 128), f32),
@@ -738,18 +789,18 @@
             vmem((REACH, 2, tile_rows + 8, 128), f32),
             vmem((PARTS, blks, 2 * STATS, 128), f32),
             vmem((2, STATS, 128), f32),
-            vmem((blks, 8, half), f32),
-            vmem((blks, half, full), bf16),
-            vmem((blks, half, full), bf16),
+            vmem((blks, 3, 8, hidden // 4), f32),
+            vmem((blks, 3, hidden // 4, full), bf16),
+            vmem((blks, 3, hidden // 4, full), bf16),
             vmem((PARTS, blks, part_px, chans), bf16),
             vmem((PARTS, 2 * part_px, full), bf16),
             vmem((PARTS, 2 * part_px, full), f32),
             vmem((PARTS, part_px, full), bf16),
             vmem((PARTS, part_px, full), bf16),
             vmem((PARTS, part_px, full), bf16),
-            dma((2,)), dma((5,)), dma((5,)), dma((blks,)), dma((blks,)), dma((PARTS, blks)), dma((PARTS, blks)),
-            dma((2, 2)), dma((2, blks)), dma((2, blks)), dma((2, blks)), dma((2, blks)),
-            dma((2, 2, blks)), dma((2, 2, blks)),
+            dma((2, 3)), dma((5,)), dma((5,)), dma((blks,)), dma((blks,)), dma((PARTS, blks)), dma((PARTS, blks)),
+            dma((2, 2)), dma((2, blks)), dma((2, blks)), dma((2, 2, blks)), dma((2, 2, blks)),
+            dma((2, 3, blks)), dma((2, 3, blks)),
             dma((PARTS, blks)), dma((PARTS, blks)), dma((PARTS,)),
             dma((PARTS, blks)), dma((PARTS, blks)), dma((PARTS, pairs)), dma((PARTS, pairs)),
             dma((PARTS, pairs, blks)), dma((PARTS, pairs, blks)), dma((PARTS, pairs)),

time: 109 us -> 98.1 us (0.90)
  Pallas kernels: 106 us -> 95 us
    pallas_call x1, Pallas kernels: 106 us -> 95 us  [fused(): pl.pallas_call(fused_kernel, in_specs=[pl.BlockSpec(memory_space=pltpu.HB...]
where the time goes in v3:
time: 98.1 us; the launch traced here: 97.9 us
  Pallas kernels  95 us (97%)
  other arithmetic  2.95 us (3%)
    pallas_call x1, Pallas kernels, fused(): pl.pallas_call(fused_kernel, in_specs=[pl.BlockSpec(memory_space=pltpu.HB...  95 us
    convert_element_type x1, other arithmetic, fused(): return result.astype(bf16)  2.95 us

profile of v3, /device:TPU:0, one launch (start us, length us, event | category | flops | bytes accessed | tf_op | source)
XLA Modules:
  0.0 97.9 jit_solution(3216793694558076557)
XLA Ops:
  0.0 95.0 %shard_map.100 = bf16[2048,256]{1,0:T(8,128)(2,1)} custom-call(bf16[64,32,256]{2,1,0:T(8,128)(2,1)} %px_hbm.1, f32[7,7,256]{2,1,0:T(8,128)} %dwk_hbm.1, f32[1,256]{1,0:T(1,128)} %bitcast.8, f32[1,256]{1,0:T(1,128)} %bitcast.9, f32[1,256]{1,0:T(1,128)} %bitcast.10, bf16[8,128]{1,0:T(8,128)(2,1)} %bitcast.7, bf16[1024,1024]{1,0:T(8,128)(2,1)} %w_in.1, ...), custom_call_target="tpu_custom_call" | custom-call | tf_op jit(solution)/shard_map/pallas_call | solution.py:768
  95.0 3.0 %fusion.2 = bf16[64,32,256]{2,1,0:T(8,128)(2,1)} fusion(bf16[64,32,256]{2,1,0:T(8,128)(2,1)} %bitcast.6, bf16[64,32,256]{2,1,0:T(8,128)(2,1)} %px_hbm.1, f32[256]{0:T(256)} %param.18, f32[256]{0:T(256)} %param.19), kind=kLoop, calls=%fused_computation.3 | loop fusion | flops 3145728 | bytes 3147776 | tf_op jit(solution)/shard_map/convert_element_type | solution.py:818

commit v4 on v3

--- a/solution.py
+++ b/solution.py
@@ -182,6 +182,7 @@
 REACH = (KS - 1) // 2
 PARTS = 4
 GROUPS = 8
+CUTS = 2
 BLOCK = 128
 STATS = 4
 
@@ -288,28 +289,35 @@
     )
 
     quarters = (2 * y + x, 2 * y + 1 - x, 2 * (1 - y) + x)
-    mine = pl.ds(pl.multiple_of(c * eighth, eighth), eighth)
-    theirs = pl.ds(pl.multiple_of((1 - c) * eighth, eighth), eighth)
     start = pl.multiple_of(quarters[0] * quarter + c * eighth, eighth)
-    weights = ((w_in, first), (w_out, second))
+    weights = tuple((src, dst, n) for src, dst in ((w_in, first), (w_out, second)) for n in range(CUTS))
+    cut = eighth // CUTS
+
+    def spot_for(k, origin, n, core):
+        begin = pl.multiple_of(core * eighth + weights[k][2] * cut, cut)
+        return weights[k][1].at[origin, n, pl.ds(begin, cut)]
+
+    def each(k):
+        return range(k * CUTS, (k + 1) * CUTS)
+
 
     def mate(part):
         return partner if part % 2 == 0 else side
 
     def own_copies(k):
-        src, dst = weights[k]
+        src, _, n = weights[k]
         for way, cond, step in ((0, z < blks - 1, 1), (1, z > 0, -1)):
             yield cond, lambda way=way, step=step: remote(
-                src.at[pl.ds(start, eighth)], dst.at[z, 0, mine],
+                src.at[pl.ds(pl.multiple_of(start + n * cut, cut), cut)], spot_for(k, z, 0, c),
                 zown_s.at[k, way], z_r.at[k, z], at_z(z + step),
             )
 
     def own_out(k):
-        for cond, make in own_copies(k):
+        for cond, make in (pair for j in each(k) for pair in own_copies(j)):
             when(cond, lambda make=make: make().start())
 
     def own_gone(k):
-        for cond, make in own_copies(k):
+        for cond, make in (pair for j in each(k) for pair in own_copies(j)):
             when(cond, lambda make=make: make().wait_send())
 
     own_out(0)
@@ -317,7 +325,7 @@
         pltpu.make_async_copy(
             src.at[pl.ds(pl.multiple_of(quarters[n] * quarter, quarter), quarter)], dst.at[z, n], own_sem.at[k, n]
         )
-        for k, (src, dst) in enumerate(weights)
+        for k, (src, dst) in enumerate(((w_in, first), (w_out, second)))
         for n in range(3)
     ]
     for copy in own:
@@ -550,25 +558,27 @@
         return ((z >= dist, lambda: z - dist, z < blks - 1, 1), (z + dist < blks, lambda: z + dist, z > 0, -1))
 
     def passed_on(dist, k):
-        block = weights[k][1]
         for cond, origin, more, step in both_ways(dist):
-            spot = lambda origin=origin: block.at[origin(), 0, mine]
+            spot = lambda origin=origin: spot_for(k, origin(), 0, c)
             yield cond & more, lambda spot=spot, origin=origin, step=step: remote(
                 spot(), spot(), zfwd_s.at[k, origin()], z_r.at[k, origin()], at_z(z + step)
             )
 
     def forward(dist, k):
-        for cond, make in passed_on(dist, k):
+        for cond, make in (pair for j in each(k) for pair in passed_on(dist, j)):
             when(cond, lambda make=make: make().start())
 
     def forwarded(dist, k):
-        for cond, make in passed_on(dist, k):
+        for cond, make in (pair for j in each(k) for pair in passed_on(dist, j)):
             when(cond, lambda make=make: make().wait_send())
 
     def take_in(dist, k):
-        block = weights[k][1]
+        for j in each(k):
+            take_piece(dist, j)
+
+    def take_piece(dist, k):
         for cond, origin, _, _ in both_ways(dist):
-            spot = lambda origin=origin: block.at[origin(), 0, mine]
+            spot = lambda origin=origin: spot_for(k, origin(), 0, c)
             when(
                 cond,
                 lambda spot=spot, origin=origin: arrived(spot(), zown_s.at[k, 0], z_r.at[k, origin()], side),
@@ -576,7 +586,7 @@
             for n, device in ((1, side), (2, partner)):
                 send(
                     lambda spot=spot, origin=origin, n=n, device=device: remote(
-                        spot(), block.at[origin(), n, mine], x_s.at[k, n - 1, origin()], x_r.at[k, n - 1, origin()],
+                        spot(), spot_for(k, origin(), n, c), x_s.at[k, n - 1, origin()], x_r.at[k, n - 1, origin()],
                         device,
                     ),
                     cond,
@@ -589,10 +599,13 @@
             )
 
     def share(dist, k):
-        block = weights[k][1]
+        for j in each(k):
+            share_piece(dist, j)
+
+    def share_piece(dist, k):
         for cond, origin, _, _ in both_ways(dist):
             for n, device in ((1, side), (2, partner)):
-                spot = lambda origin=origin, n=n: block.at[origin(), n, mine]
+                spot = lambda origin=origin, n=n: spot_for(k, origin(), n, c)
                 when(
                     cond,
                     lambda spot=spot, origin=origin, n=n, device=device: arrived(
@@ -606,15 +619,22 @@
                     cond,
                 )
 
-    def ready():
+    shift = jnp.where(z < blks // 2, 0, 1)
+    far = jnp.where(z < blks // 2, blks - 1, 0)
+
+    def hold(other):
+        for k in range(len(weights)):
+            for n in range(3):
+                arrived(spot_for(k, other, n, 1 - c), c_s.at[k, n, other], c_r.at[k, n, other], sibling)
+
+    def early():
         for copy in own:
             copy.wait()
         for step in range(1, blks):
             other = (z + step) % blks
             arrived(b_all.at[other], bias_s.at[step], bias_r.at[other], at_z(other))
-            for k in range(2):
-                for n in range(3):
-                    arrived(weights[k][1].at[other, n, theirs], c_s.at[k, n, other], c_r.at[k, n, other], sibling)
+        for i in range(blks - 1):
+            pl.when(i + shift != z)(lambda i=i: hold(i + shift))
         wide_rows = quarter // 128
         for o in range(blks):
             for n in range(3):
@@ -623,37 +643,33 @@
                         b_all[o, pl.ds(quarters[n] * wide_rows + k, 1), :], (8, 128)
                     )
 
-    def feed(part):
+    def late():
+        hold(far)
+
+    def term_of(part, o):
+        def hidden_of(n):
+            pre_act = lax.dot_general(
+                act[part], first[o, n], (((1,), (1,)), ((), ())), preferred_element_type=jnp.float32
+            )
+            pre_act = pre_act + bias[o, n, 0:1, :]
+            return (0.5 * pre_act * (1.0 + lax.erf(pre_act * 0.7071067811865476))).astype(jnp.bfloat16)
+
+        return sum(
+            jnp.dot(hidden_of(n), second[o, n], preferred_element_type=jnp.float32) for n in (0, 1 + part % 2)
+        )
+
+    def begin_feed(part):
         for step in range(blks):
             other = (z + step) % blks
             arrived(
                 act.at[part, pl.ds(part_px, part_px), columns(other)], y_s.at[part, step], y_r.at[part, other], mate(part)
             )
-
-        def hidden_of(o, n):
-            pre_act = lax.dot_general(
-                act[part], first[o, n], (((1,), (1,)), ((), ())), preferred_element_type=jnp.float32
-            )
-            pre_act = pre_act + bias[o, n, 0:1, :]
-            return (0.5 * pre_act * (1.0 + lax.erf(pre_act * 0.7071067811865476))).astype(jnp.bfloat16)
-
-        def body(o, _):
-            term = sum(
-                jnp.dot(hidden_of(o, n), second[o, n], preferred_element_type=jnp.float32)
-                for n in (0, 1 + part % 2)
-            )
-
-            @pl.when(o == 0)
-            def _():
-                acc[part] = term
-
-            @pl.when(o > 0)
-            def _():
-                acc[part] += term
-
-            return 0
-
-        lax.fori_loop(0, blks, body, 0)
+        for i in range(blks - 1):
+            term = term_of(part, i + shift)
+            acc[part] = term if i == 0 else acc[part] + term
+
+    def end_feed(part):
+        acc[part] = acc[part] + term_of(part, far)
         for n in range(per_blk):
             rows = slice(n * group_px, (n + 1) * group_px)
             p_send[part, rows, :] = acc[part, part_px + n * group_px : part_px + (n + 1) * group_px, :].astype(
@@ -737,14 +753,19 @@
     share(3, 1)
     swap_rows(2)
     regroup(3)
-    ready()
-    feed(0)
+    early()
+    begin_feed(0)
+    late()
+    end_feed(0)
+    begin_feed(1)
+    end_feed(1)
     swap_rows(3)
-    feed(1)
     give_back(0)
-    feed(2)
+    begin_feed(2)
+    end_feed(2)
     give_back(1)
-    feed(3)
+    begin_feed(3)
+    end_feed(3)
     give_back(2)
     give_back(3)
     for part in range(PARTS):
@@ -799,8 +820,8 @@
             vmem((PARTS, part_px, full), bf16),
             vmem((PARTS, part_px, full), bf16),
             dma((2, 3)), dma((5,)), dma((5,)), dma((blks,)), dma((blks,)), dma((PARTS, blks)), dma((PARTS, blks)),
-            dma((2, 2)), dma((2, blks)), dma((2, blks)), dma((2, 2, blks)), dma((2, 2, blks)),
-            dma((2, 3, blks)), dma((2, 3, blks)),
+            dma((2 * CUTS, 2)), dma((2 * CUTS, blks)), dma((2 * CUTS, blks)),
+            dma((2 * CUTS, 2, blks)), dma((2 * CUTS, 2, blks)), dma((2 * CUTS, 3, blks)), dma((2 * CUTS, 3, blks)),
             dma((PARTS, blks)), dma((PARTS, blks)), dma((PARTS,)),
             dma((PARTS, blks)), dma((PARTS, blks)), dma((PARTS, pairs)), dma((PARTS, pairs)),
             dma((PARTS, pairs, blks)), dma((PARTS, pairs, blks)), dma((PARTS, pairs)),

time: 98.1 us -> 94.4 us (0.962)
  Pallas kernels: 95 us -> 91.3 us
    pallas_call x1, Pallas kernels: 95 us -> 91.3 us  [fused(): pl.pallas_call(fused_kernel, in_specs=[pl.BlockSpec(memory_space=pltpu.HB...]
where the time goes in v4:
time: 94.4 us; the launch traced here: 94.2 us
  Pallas kernels  91.3 us (97%)
  other arithmetic  2.95 us (3%)
    pallas_call x1, Pallas kernels, fused(): pl.pallas_call(fused_kernel, in_specs=[pl.BlockSpec(memory_space=pltpu.HB...  91.3 us
    convert_element_type x1, other arithmetic, fused(): return result.astype(bf16)  2.95 us

profile of v4, /device:TPU:0, one launch (start us, length us, event | category | flops | bytes accessed | tf_op | source)
XLA Modules:
  0.0 94.2 jit_solution(13765865981438643957)
XLA Ops:
  0.0 91.3 %shard_map.100 = bf16[2048,256]{1,0:T(8,128)(2,1)} custom-call(bf16[64,32,256]{2,1,0:T(8,128)(2,1)} %px_hbm.1, f32[7,7,256]{2,1,0:T(8,128)} %dwk_hbm.1, f32[1,256]{1,0:T(1,128)} %bitcast.8, f32[1,256]{1,0:T(1,128)} %bitcast.9, f32[1,256]{1,0:T(1,128)} %bitcast.10, bf16[8,128]{1,0:T(8,128)(2,1)} %bitcast.7, bf16[1024,1024]{1,0:T(8,128)(2,1)} %w_in.1, ...), custom_call_target="tpu_custom_call" | custom-call | tf_op jit(solution)/shard_map/pallas_call | solution.py:789
  91.3 3.0 %fusion.2 = bf16[64,32,256]{2,1,0:T(8,128)(2,1)} fusion(bf16[64,32,256]{2,1,0:T(8,128)(2,1)} %bitcast.6, bf16[64,32,256]{2,1,0:T(8,128)(2,1)} %px_hbm.1, f32[256]{0:T(256)} %param.18, f32[256]{0:T(256)} %param.19), kind=kLoop, calls=%fused_computation.3 | loop fusion | flops 3145728 | bytes 3147776 | tf_op jit(solution)/shard_map/convert_element_type | solution.py:839
